TPU v7x, 32 devices: a whole 2x2x4 slice. The times are simulated.
32 devices in a mesh: seq: 4 (over y, core), fsdp: 8 (over z, x).
Axes of the slice: x: 2, y: 2, z: 4, core: 2. Of those that a mesh axis runs over, the one named last changes fastest.
Arguments:
- tokens: bfloat16 [32, 200, 768], P(('fsdp', 'seq')), may hold values from -6 to 6
- key_mask: int32 [32, 200], P('fsdp'), may hold values from 0 to 1, as said below
- expert_ids: int32 [32, 200, 2], P(('fsdp', 'seq')), may hold values from 0 to 3, all different within a row; in each aligned block of 200 rows (0 to 199, 200 to 399, ..., all dimensions but the last counted through in order) at most 142 rows name the same one
- cotangent: bfloat16 [32, 200, 768], P(('fsdp', 'seq')), may hold values from -6 to 6
- norm1_gain: bfloat16 [768], P('fsdp'), may hold values from 0.5 to 1.5
- norm1_bias: bfloat16 [768], P('fsdp'), may hold values from -1 to 1
- w_qkv: bfloat16 [768, 2304], P('fsdp'), may hold values from -0.21875 to 0.21875
- w_proj: bfloat16 [768, 768], P('fsdp'), may hold values from -1.75 to 1.75
- proj_bias: bfloat16 [768], P('fsdp'), may hold values from -1 to 1
- norm2_gain: bfloat16 [768], P('fsdp'), may hold values from 0.5 to 1.5
- norm2_bias: bfloat16 [768], P('fsdp'), may hold values from -1 to 1
- w_router: bfloat16 [768, 4], P('fsdp'), may hold values from -0.15625 to 0.15625
- w_in: bfloat16 [4, 768, 3072], P(None, 'fsdp'), may hold values from -0.21875 to 0.21875
- b_in: bfloat16 [4, 3072], P(None, 'fsdp'), may hold values from -1 to 1
- w_out: bfloat16 [4, 3072, 768], P(None, 'fsdp'), may hold values from -0.3125 to 0.3125
- b_out: bfloat16 [4, 768], P(None, 'fsdp'), may hold values from -1 to 1
Outputs:
- mixed: bfloat16 [32, 200, 768], P(('fsdp', 'seq'))
- token_grad: bfloat16 [32, 200, 768], P(('fsdp', 'seq'))
- norm1_gain_grad: float32 [768], P('fsdp')
- norm1_bias_grad: float32 [768], P('fsdp')
- w_qkv_grad: float32 [768, 2304], P('fsdp')
- w_proj_grad: float32 [768, 768], P('fsdp')
- proj_bias_grad: float32 [768], P('fsdp')
- norm2_gain_grad: float32 [768], P('fsdp')
- norm2_bias_grad: float32 [768], P('fsdp')
- w_router_grad: float32 [768, 4], P('fsdp')
- w_in_grad: float32 [4, 768, 3072], P(None, 'fsdp')
- b_in_grad: float32 [4, 3072], P(None, 'fsdp')
- w_out_grad: float32 [4, 3072, 768], P(None, 'fsdp')
- b_out_grad: float32 [4, 768], P(None, 'fsdp')
Inputs may be any that keep to these rules, and one draw needn't show every extreme that they name: `expert_ids`: each token names two different experts. Among the 200 tokens of one device (aligned blocks of rows) no expert is named more than 142 times, and some expert of some device is named exactly 142 times. `key_mask`: each image's mask is 1 on a prefix of 160 to 200 tokens and 0 after it; both ends occur.
All inputs are finite; a program needn't handle non-finite values.
Results may differ from a plain program's by a relative error of at most 0.018.
Values may be sent and summed in bfloat16 or wider, within the bound.
A program may use at most 320 MiB of HBM per device.

v0:
```python
import functools

import jax
import jax.numpy as jnp
from jax import lax
from jax.experimental import pallas as pl
from jax.experimental.pallas import tpu as pltpu
from jax.sharding import PartitionSpec as P

HEADS = 12
CAP = 142


epsilon = 1e-06
masked_score = -1e30


def norm_rows(values, gain, offset):
    center = values - jnp.mean(values, axis=-1, keepdims=True)
    spread = jnp.mean(center * center, axis=-1, keepdims=True)
    return center * lax.rsqrt(spread + epsilon) * gain + offset


def softmax_rows(values):
    shifted = jnp.exp(values - jnp.max(values, axis=-1, keepdims=True))
    return shifted / jnp.sum(shifted, axis=-1, keepdims=True)


def exact_gelu(values):
    return jax.nn.gelu(values, approximate=False)


def expert_slots(chosen, experts):
    flat_ids = chosen.reshape(-1)
    onehot = (flat_ids[:, None] == jnp.arange(experts, dtype=jnp.int32)[None, :]).astype(jnp.int32)
    ranks = jnp.cumsum(onehot, axis=0, dtype=jnp.int32)
    slot_pos = jnp.sum(onehot * ranks, axis=1, dtype=jnp.int32) - 1
    return (flat_ids, slot_pos)


def gather_weights_plan(
    tokens,
    key_mask,
    expert_ids,
    cotangent,
    norm1_gain,
    norm1_bias,
    w_qkv,
    w_proj,
    proj_bias,
    norm2_gain,
    norm2_bias,
    w_router,
    w_in,
    b_in,
    w_out,
    b_out,
):
    images, seq_len, width = tokens.shape
    experts = w_in.shape[0]
    head_dim = width // HEADS
    scaling = head_dim ** (-0.5)
    row_count = images * seq_len
    dense_set = (
        lax.all_gather(norm1_gain, "fsdp", axis=0, tiled=True),
        lax.all_gather(norm1_bias, "fsdp", axis=0, tiled=True),
        lax.all_gather(w_qkv, "fsdp", axis=0, tiled=True),
        lax.all_gather(w_proj, "fsdp", axis=0, tiled=True),
        lax.all_gather(proj_bias, "fsdp", axis=0, tiled=True),
        lax.all_gather(norm2_gain, "fsdp", axis=0, tiled=True),
        lax.all_gather(norm2_bias, "fsdp", axis=0, tiled=True),
        lax.all_gather(w_router, "fsdp", axis=0, tiled=True),
    )
    gain_first = dense_set[0].astype(jnp.float32)
    bias_first = dense_set[1].astype(jnp.float32)
    full_qkv = dense_set[2]
    full_proj = dense_set[3]
    bias_proj = dense_set[4].astype(jnp.float32)
    gain_second = dense_set[5].astype(jnp.float32)
    bias_second = dense_set[6].astype(jnp.float32)
    full_router = dense_set[7]
    expert_set = (
        lax.all_gather(w_in, "fsdp", axis=1, tiled=True),
        lax.all_gather(b_in, "fsdp", axis=1, tiled=True),
        lax.all_gather(w_out, "fsdp", axis=1, tiled=True),
        lax.all_gather(b_out, "fsdp", axis=1, tiled=True),
    )
    inner_weight = expert_set[0]
    inner_bias = expert_set[1].astype(jnp.float32)
    outer_weight = expert_set[2]
    outer_bias = expert_set[3].astype(jnp.float32)
    own_mask = lax.dynamic_slice_in_dim(key_mask, lax.axis_index("seq") * images, images, 0)
    keep_rows = own_mask.reshape(row_count, 1).astype(jnp.float32)
    usable = (key_mask > 0)[:, None, None, :]
    flat_tokens = tokens.astype(jnp.float32).reshape(row_count, width)
    normed_in = norm_rows(flat_tokens, gain_first, bias_first).astype(jnp.bfloat16)
    mixed_qkv = jnp.dot(normed_in, full_qkv, preferred_element_type=jnp.float32).astype(
        jnp.bfloat16
    )
    mixed_qkv = mixed_qkv.reshape(images, seq_len, 3, HEADS, head_dim)
    head_qkv = lax.all_to_all(mixed_qkv, "seq", split_axis=3, concat_axis=0, tiled=True)
    queries = head_qkv[:, :, 0]
    key_rows = head_qkv[:, :, 1]
    value_rows = head_qkv[:, :, 2]

    def score_block():
        raw = (
            jnp.einsum("gahd,gbhd->ghab", queries, key_rows, preferred_element_type=jnp.float32)
            * scaling
        )
        return jnp.where(usable, raw, masked_score)

    scores = score_block()
    row_top = jnp.max(scores, axis=-1, keepdims=True)
    shifted = jnp.exp(scores - row_top)
    row_total = jnp.sum(shifted, axis=-1, keepdims=True)
    attn_probs = (shifted / row_total).astype(jnp.bfloat16)
    log_total = row_top + jnp.log(row_total)
    head_out = jnp.einsum(
        "ghab,gbhd->gahd", attn_probs, value_rows, preferred_element_type=jnp.float32
    ).astype(jnp.bfloat16)
    attended = lax.all_to_all(head_out, "seq", split_axis=0, concat_axis=2, tiled=True).reshape(
        row_count, width
    )
    middle = (
        flat_tokens + jnp.dot(attended, full_proj, preferred_element_type=jnp.float32) + bias_proj
    )
    normed_mid = norm_rows(middle, gain_second, bias_second).astype(jnp.bfloat16)
    routing = softmax_rows(jnp.dot(normed_mid, full_router, preferred_element_type=jnp.float32))
    chosen = expert_ids.reshape(row_count, 2)
    flat_ids, slot_pos = expert_slots(chosen, experts)
    gating = jnp.take_along_axis(routing, chosen, axis=1)
    buffer = (
        jnp.zeros((experts, CAP, width), jnp.bfloat16)
        .at[flat_ids, slot_pos]
        .set(jnp.repeat(normed_mid, 2, axis=0))
    )
    pre_act = (
        jnp.einsum("ecd,edf->ecf", buffer, inner_weight, preferred_element_type=jnp.float32)
        + inner_bias[:, None, :]
    )
    activated = exact_gelu(pre_act).astype(jnp.bfloat16)
    expert_out = (
        jnp.einsum("ecf,efd->ecd", activated, outer_weight, preferred_element_type=jnp.float32)
        + outer_bias[:, None, :]
    )
    picked = expert_out[flat_ids, slot_pos].reshape(row_count, 2, width)
    mixture = jnp.sum(gating[:, :, None] * picked, axis=1)
    mixed = (keep_rows * (middle + mixture)).astype(jnp.bfloat16).reshape(images, seq_len, width)
    grad_out = cotangent.astype(jnp.float32).reshape(row_count, width) * keep_rows
    grad_gate = jnp.sum(grad_out[:, None, :] * picked, axis=2)
    grad_picked = (
        (gating[:, :, None] * grad_out[:, None, :])
        .astype(jnp.bfloat16)
        .reshape(2 * row_count, width)
    )
    grad_expert_out = (
        jnp.zeros((experts, CAP, width), jnp.bfloat16).at[flat_ids, slot_pos].set(grad_picked)
    )
    grad_outer_bias = jnp.sum(grad_expert_out, axis=1, dtype=jnp.float32)
    hidden_pre = (
        jnp.einsum("ecd,edf->ecf", buffer, inner_weight, preferred_element_type=jnp.float32)
        + inner_bias[:, None, :]
    )
    hidden_act = exact_gelu(hidden_pre).astype(jnp.bfloat16)
    grad_outer_weight = jnp.einsum(
        "ecf,ecd->efd", hidden_act, grad_expert_out, preferred_element_type=jnp.float32
    )
    grad_act = jnp.einsum(
        "ecd,efd->ecf", grad_expert_out, outer_weight, preferred_element_type=jnp.float32
    )
    gelu_pull = jax.vjp(exact_gelu, hidden_pre)[1]
    grad_pre = gelu_pull(grad_act)[0].astype(jnp.bfloat16)
    grad_inner_bias = jnp.sum(grad_pre, axis=1, dtype=jnp.float32)
    grad_inner_weight = jnp.einsum(
        "ecd,ecf->edf", buffer, grad_pre, preferred_element_type=jnp.float32
    )
    grad_buffer = jnp.einsum(
        "ecf,edf->ecd", grad_pre, inner_weight, preferred_element_type=jnp.float32
    )
    grad_rows = jnp.sum(grad_buffer[flat_ids, slot_pos].reshape(row_count, 2, width), axis=1)
    expert_range = jnp.arange(experts, dtype=jnp.int32)[None, None, :]
    grad_route = jnp.sum(
        grad_gate[:, :, None] * (chosen[:, :, None] == expert_range).astype(jnp.float32), axis=1
    )
    grad_logits = (
        routing * (grad_route - jnp.sum(routing * grad_route, axis=-1, keepdims=True))
    ).astype(jnp.bfloat16)
    grad_router = jnp.einsum(
        "nd,ne->de", normed_mid, grad_logits, preferred_element_type=jnp.float32
    )
    grad_normed_mid = grad_rows + jnp.einsum(
        "ne,de->nd", grad_logits, full_router, preferred_element_type=jnp.float32
    )
    second_pull = jax.vjp(norm_rows, middle, gain_second, bias_second)[1]
    grad_mid_norm, grad_gain_second, grad_bias_second = second_pull(grad_normed_mid)
    grad_middle = grad_out + grad_mid_norm
    grad_proj = grad_middle.astype(jnp.bfloat16)
    grad_bias_proj = jnp.sum(grad_proj, axis=0, dtype=jnp.float32)
    grad_proj_weight = jnp.einsum(
        "nd,ne->de", attended, grad_proj, preferred_element_type=jnp.float32
    )
    grad_attended = jnp.einsum(
        "ne,de->nd", grad_proj, full_proj, preferred_element_type=jnp.float32
    ).astype(jnp.bfloat16)
    grad_head_out = lax.all_to_all(
        grad_attended.reshape(images, seq_len, HEADS, head_dim),
        "seq",
        split_axis=2,
        concat_axis=0,
        tiled=True,
    )
    recomputed = jnp.exp(score_block() - log_total)
    grad_values = jnp.einsum(
        "ghab,gahd->gbhd",
        recomputed.astype(jnp.bfloat16),
        grad_head_out,
        preferred_element_type=jnp.float32,
    )
    grad_probs = jnp.einsum(
        "gahd,gbhd->ghab", grad_head_out, value_rows, preferred_element_type=jnp.float32
    )
    grad_scores = (
        recomputed * (grad_probs - jnp.sum(recomputed * grad_probs, axis=-1, keepdims=True))
    ).astype(jnp.bfloat16)
    grad_queries = (
        jnp.einsum("ghab,gbhd->gahd", grad_scores, key_rows, preferred_element_type=jnp.float32)
        * scaling
    )
    grad_keys = (
        jnp.einsum("ghab,gahd->gbhd", grad_scores, queries, preferred_element_type=jnp.float32)
        * scaling
    )
    grad_head_qkv = jnp.stack([grad_queries, grad_keys, grad_values], axis=2).astype(jnp.bfloat16)
    grad_qkv = lax.all_to_all(
        grad_head_qkv, "seq", split_axis=0, concat_axis=3, tiled=True
    ).reshape(row_count, 3 * width)
    grad_qkv_weight = jnp.einsum(
        "nd,ne->de", normed_in, grad_qkv, preferred_element_type=jnp.float32
    )
    grad_normed_in = jnp.einsum("ne,de->nd", grad_qkv, full_qkv, preferred_element_type=jnp.float32)
    first_pull = jax.vjp(norm_rows, flat_tokens, gain_first, bias_first)[1]
    grad_first, grad_gain_first, grad_bias_first = first_pull(grad_normed_in)
    token_grad = (grad_middle + grad_first).astype(jnp.bfloat16).reshape(images, seq_len, width)
    shares = (
        lax.psum_scatter(grad_gain_first, "fsdp", scatter_dimension=0, tiled=True),
        lax.psum_scatter(grad_bias_first, "fsdp", scatter_dimension=0, tiled=True),
        lax.psum_scatter(grad_qkv_weight, "fsdp", scatter_dimension=0, tiled=True),
        lax.psum_scatter(grad_proj_weight, "fsdp", scatter_dimension=0, tiled=True),
        lax.psum_scatter(grad_bias_proj, "fsdp", scatter_dimension=0, tiled=True),
        lax.psum_scatter(grad_gain_second, "fsdp", scatter_dimension=0, tiled=True),
        lax.psum_scatter(grad_bias_second, "fsdp", scatter_dimension=0, tiled=True),
        lax.psum_scatter(grad_router, "fsdp", scatter_dimension=0, tiled=True),
        lax.psum_scatter(grad_inner_weight, "fsdp", scatter_dimension=1, tiled=True),
        lax.psum_scatter(grad_inner_bias, "fsdp", scatter_dimension=1, tiled=True),
        lax.psum_scatter(grad_outer_weight, "fsdp", scatter_dimension=1, tiled=True),
        lax.psum_scatter(grad_outer_bias, "fsdp", scatter_dimension=1, tiled=True),
    )
    parted = (
        lax.psum_scatter(
            shares[0].astype(jnp.bfloat16), "seq", scatter_dimension=0, tiled=True
        ).astype(jnp.float32),
        lax.psum_scatter(
            shares[1].astype(jnp.bfloat16), "seq", scatter_dimension=0, tiled=True
        ).astype(jnp.float32),
        lax.psum_scatter(
            shares[2].astype(jnp.bfloat16), "seq", scatter_dimension=0, tiled=True
        ).astype(jnp.float32),
        lax.psum_scatter(
            shares[3].astype(jnp.bfloat16), "seq", scatter_dimension=0, tiled=True
        ).astype(jnp.float32),
        lax.psum_scatter(
            shares[4].astype(jnp.bfloat16), "seq", scatter_dimension=0, tiled=True
        ).astype(jnp.float32),
        lax.psum_scatter(
            shares[5].astype(jnp.bfloat16), "seq", scatter_dimension=0, tiled=True
        ).astype(jnp.float32),
        lax.psum_scatter(
            shares[6].astype(jnp.bfloat16), "seq", scatter_dimension=0, tiled=True
        ).astype(jnp.float32),
        lax.psum_scatter(
            shares[7].astype(jnp.bfloat16), "seq", scatter_dimension=0, tiled=True
        ).astype(jnp.float32),
        lax.psum_scatter(
            shares[8].astype(jnp.bfloat16), "seq", scatter_dimension=1, tiled=True
        ).astype(jnp.float32),
        lax.psum_scatter(
            shares[9].astype(jnp.bfloat16), "seq", scatter_dimension=1, tiled=True
        ).astype(jnp.float32),
        lax.psum_scatter(
            shares[10].astype(jnp.bfloat16), "seq", scatter_dimension=1, tiled=True
        ).astype(jnp.float32),
        lax.psum_scatter(
            shares[11].astype(jnp.bfloat16), "seq", scatter_dimension=1, tiled=True
        ).astype(jnp.float32),
    )
    totals = (
        lax.all_gather(parted[0].astype(jnp.bfloat16), "seq", axis=0, tiled=True).astype(
            jnp.float32
        ),
        lax.all_gather(parted[1].astype(jnp.bfloat16), "seq", axis=0, tiled=True).astype(
            jnp.float32
        ),
        lax.all_gather(parted[2].astype(jnp.bfloat16), "seq", axis=0, tiled=True).astype(
            jnp.float32
        ),
        lax.all_gather(parted[3].astype(jnp.bfloat16), "seq", axis=0, tiled=True).astype(
            jnp.float32
        ),
        lax.all_gather(parted[4].astype(jnp.bfloat16), "seq", axis=0, tiled=True).astype(
            jnp.float32
        ),
        lax.all_gather(parted[5].astype(jnp.bfloat16), "seq", axis=0, tiled=True).astype(
            jnp.float32
        ),
        lax.all_gather(parted[6].astype(jnp.bfloat16), "seq", axis=0, tiled=True).astype(
            jnp.float32
        ),
        lax.all_gather(parted[7].astype(jnp.bfloat16), "seq", axis=0, tiled=True).astype(
            jnp.float32
        ),
        lax.all_gather(parted[8].astype(jnp.bfloat16), "seq", axis=1, tiled=True).astype(
            jnp.float32
        ),
        lax.all_gather(parted[9].astype(jnp.bfloat16), "seq", axis=1, tiled=True).astype(
            jnp.float32
        ),
        lax.all_gather(parted[10].astype(jnp.bfloat16), "seq", axis=1, tiled=True).astype(
            jnp.float32
        ),
        lax.all_gather(parted[11].astype(jnp.bfloat16), "seq", axis=1, tiled=True).astype(
            jnp.float32
        ),
    )
    return (
        mixed,
        token_grad,
        totals[0],
        totals[1],
        totals[2],
        totals[3],
        totals[4],
        totals[5],
        totals[6],
        totals[7],
        totals[8],
        totals[9],
        totals[10],
        totals[11],
    )


MESH = pl.DeviceIdType.MESH
NT = (((1,), (1,)), ((), ()))
TN = (((0,), (0,)), ((), ()))


def dot(a, b):
    return jnp.dot(a, b, preferred_element_type=jnp.float32)


class Place:
    def __init__(self, planes):
        self.planes = planes
        s, f = lax.axis_index("seq"), lax.axis_index("fsdp")
        self.y, self.c, self.z, self.x = s // 2, s % 2, f // 2, f % 2

    def at(self, y, c, z, x):
        return (y * 2 + c, z * 2 + x)

    def other_core(self):
        return self.at(self.y, 1 - self.c, self.z, self.x)

    def other_x(self):
        return self.at(self.y, self.c, self.z, 1 - self.x)

    def other_y(self):
        return self.at(1 - self.y, self.c, self.z, self.x)

    def level(self, k):
        return self.at(self.y, self.c, lax.rem(self.z + k + self.planes, self.planes), self.x)


def greet(partners):
    barrier = pltpu.get_barrier_semaphore()
    for partner in partners:
        pl.semaphore_signal(barrier, inc=1, device_id=partner, device_id_type=MESH)
    pl.semaphore_wait(barrier, len(partners))


def nearest(place, i):
    level = 0
    for z in range(place.planes):
        order = sorted(range(place.planes), key=lambda other: (abs(other - z), other))
        for at in range(place.planes):
            level = level + jnp.where((place.z == z) & (i == at), order[at], 0)
    return level


def expert_kernel(
    planes,
    own,
    rows,
    real,
    normed_ref,
    grads_all_ref,
    inner_ref,
    outer_all_ref,
    bias_all_ref,
    small_ref,
    mix_out_ref,
    out_ref,
    inner_grad_ref,
    outer_grad_ref,
    bias_grad_ref,
    router_grad_ref,
    grads_ref,
    mix_ref,
    outer_ref,
    inner_t_ref,
    outer_t_ref,
    router_ref,
    router_t_ref,
    tokens,
    part,
    from_core,
    from_x,
    from_z,
    hidden,
    hidden_grad,
    logit_grad,
    inner_acc,
    outer_acc,
    outer_sem,
    grads_sem,
    mix_sem,
    z_send,
    z_recv,
    x_send,
    x_recv,
    c_send,
    c_recv,
    sum_c_send,
    sum_c_recv,
    sum_x_send,
    sum_x_recv,
    sum_z_send,
    sum_z_recv,
):
    f32, bf16 = jnp.float32, jnp.bfloat16
    place = Place(planes)
    y, c, z, x = place.y, place.c, place.z, place.x
    width = inner_ref.shape[0]
    lanes = inner_ref.shape[1] // own
    first = real % 16

    def remote(src, dst, send, recv, device):
        return pltpu.make_async_remote_copy(
            src_ref=src, dst_ref=dst, send_sem=send, recv_sem=recv, device_id=device, device_id_type=MESH
        )

    def slot(buffer, level, at, count=1):
        return buffer.at[level, pl.ds(at * rows, count * rows)]

    def up_copy(level):
        here = slot(tokens, level, 0)
        return remote(here, here, z_send.at[0, level], z_recv.at[0, level], place.at(y, c, z + 1, x))

    def down_copy(level):
        here = slot(tokens, level, 0)
        return remote(here, here, z_send.at[1, level], z_recv.at[1, level], place.at(y, c, z - 1, x))

    def x_copy(level):
        return remote(
            slot(tokens, level, 0), slot(tokens, level, 2), x_send.at[level], x_recv.at[level], place.other_x()
        )

    def c_copy(level, r):
        return remote(
            slot(tokens, level, 2 * r),
            slot(tokens, level, 2 * r + 1),
            c_send.at[level, r],
            c_recv.at[level, r],
            place.other_core(),
        )

    def sum_c_copy(level, r):
        return remote(
            slot(part, level, 2 * r + 1),
            slot(from_core, level, r),
            sum_c_send.at[level, r],
            sum_c_recv.at[level, r],
            place.other_core(),
        )

    def sum_x_copy(level):
        return remote(
            slot(part, level, 2), from_x.at[level], sum_x_send.at[level], sum_x_recv.at[level], place.other_x()
        )

    def sum_z_copy(level, source):
        return remote(
            slot(part, level, 0),
            from_z.at[source],
            sum_z_send.at[level],
            sum_z_recv.at[source],
            place.at(y, c, level, x),
        )

    partners = [place.other_core(), place.other_x()] + [place.level(k) for k in range(1, planes)]
    greet(partners)
    tokens[z, 0:rows, :] = normed_ref[...]

    @pl.when(z < planes - 1)
    def _():
        up_copy(z).start()

    @pl.when(z > 0)
    def _():
        down_copy(z).start()

    c_copy(z, 0).start()
    x_copy(z).start()
    def grads_load(level):
        return pltpu.make_async_copy(grads_all_ref.at[level], grads_ref.at[level], grads_sem.at[level])

    def mix_store(level, r):
        here = pl.ds(pl.multiple_of(2 * r * rows, 16), 2 * rows)
        return pltpu.make_async_copy(mix_ref.at[level, here], mix_out_ref.at[level, here], mix_sem.at[level, r])

    for i in range(planes):
        grads_load(nearest(place, i)).start()
    loads = [
        pltpu.make_async_copy(
            outer_all_ref.at[c * own + i], outer_ref.at[pl.ds(i * lanes, lanes)], outer_sem.at[i]
        )
        for i in range(own)
    ]
    for load in loads:
        load.start()
    inner_t_ref[...] = jnp.transpose(inner_ref[...])
    place_row = lax.broadcasted_iota(jnp.int32, (128, 128), 0)
    place_lane = lax.broadcasted_iota(jnp.int32, (128, 128), 1)
    take = (place_row - (5 + 2 * own) == place_lane - first) & (place_lane >= first)
    take = take & (place_lane < first + 2 * own)
    router = dot(small_ref[...], take.astype(bf16))
    router_ref[...] = router.astype(bf16)
    router_t_ref[...] = jnp.transpose(router).astype(bf16)
    inner_acc[...] = jnp.zeros_like(inner_acc)
    outer_acc[...] = jnp.zeros_like(outer_acc)
    bias_grad_ref[...] = jnp.zeros_like(bias_grad_ref)
    router_grad_ref[...] = jnp.zeros_like(router_grad_ref)
    for load in loads:
        load.wait()
    outer_t_ref[...] = jnp.transpose(outer_ref[...])

    def hop(h):
        @pl.when(z >= h)
        def _():
            up_copy(z - h).wait_recv()

            @pl.when(z < planes - 1)
            def _():
                up_copy(z - h).start()

            x_copy(z - h).start()
            c_copy(z - h, 0).start()

        @pl.when(z + h < planes)
        def _():
            down_copy(z + h).wait_recv()

            @pl.when(z > 0)
            def _():
                down_copy(z + h).start()

            x_copy(z + h).start()
            c_copy(z + h, 0).start()

    def tiles(level, r):
        here = pl.ds(pl.multiple_of(2 * r * rows, 16), 2 * rows)
        normed, grad_out = tokens[level, here, :], grads_ref[level, here, :]
        select = []
        for t in range(2):
            last = pl.ds(pl.multiple_of((2 * r + t) * rows + real - first, 16), 16)
            chosen = grads_ref[level, last, :256].astype(f32)
            chosen = jnp.concatenate([chosen, jnp.zeros((112, 256), f32)], axis=0)
            select.append(jnp.transpose(chosen)[:rows])
        select = jnp.concatenate(select, axis=0)
        lane = lax.broadcasted_iota(jnp.int32, select.shape, 1)
        named = (lane >= first) & (lane < first + 2 * own)
        select = jnp.where(named, select, 0.0)
        logits = jnp.where(named, dot(normed, router_ref[...]), -1e30)
        routing = jnp.exp(logits - jnp.max(logits, axis=1, keepdims=True))
        routing = routing / jnp.sum(routing, axis=1, keepdims=True)
        gates = routing * select
        gate_grads = jnp.zeros_like(gates)
        all_pre = dot(normed, inner_ref[...])
        all_grad_act = dot(grad_out, outer_t_ref[...])
        for i in range(own):
            mine = lane == first + c * own + i
            units = slice(i * lanes, (i + 1) * lanes)
            gate = jnp.sum(jnp.where(mine, gates, 0.0), axis=1, keepdims=True)
            bias = jnp.where(c == 0, bias_all_ref[i : i + 1, :], bias_all_ref[own + i : own + i + 1, :])
            pre = all_pre[:, units] + bias.astype(f32)
            grad_act = all_grad_act[:, units]
            cdf = 0.5 * (1.0 + lax.erf(pre * (0.5**0.5)))
            act = pre * cdf
            hidden[here, units] = (gate * act).astype(bf16)
            gate_grad = jnp.sum(act * grad_act, axis=1, keepdims=True)
            gate_grads = gate_grads + jnp.where(mine, gate_grad * select, 0.0)
            slope = cdf + pre * jnp.exp(-0.5 * pre * pre) * 0.3989422804014327
            grad_pre = gate * grad_act * slope
            bias_grad_ref[0:1, units] += jnp.sum(grad_pre, axis=0, keepdims=True)
            hidden_grad[here, units] = grad_pre.astype(bf16)
        grad_logits = routing * (gate_grads - jnp.sum(routing * gate_grads, axis=1, keepdims=True))
        logit_grad[here, :] = grad_logits.astype(bf16)
        mix_ref[level, here, :] = dot(hidden[here, :], outer_ref[...]).astype(bf16)
        row_grad = dot(hidden_grad[here, :], inner_t_ref[...])
        row_grad = row_grad + dot(logit_grad[here, :], router_t_ref[...])
        part[level, here, :] = row_grad.astype(bf16)

    def across_sum(level):
        sum_c_copy(level, 1).wait_recv()
        here = slice(2 * rows, 3 * rows)
        total = part[level, here, :].astype(f32) + from_core[level, rows : 2 * rows, :].astype(f32)
        part[level, here, :] = total.astype(bf16)
        sum_x_copy(level).start()

    def level_sum(level):
        sum_c_copy(level, 0).wait_recv()
        sum_x_copy(level).wait_recv()
        total = part[level, 0:rows, :].astype(f32) + from_core[level, 0:rows, :].astype(f32)
        total = total + from_x[level].astype(f32)
        part[level, 0:rows, :] = total.astype(bf16)

    def weight_grads(level):
        for j in range(width // 256):
            some = slice(j * 256, (j + 1) * 256)
            outer_acc[some, :] += lax.dot_general(
                hidden[:, some], grads_ref[level], TN, preferred_element_type=f32
            )
            inner_acc[some, :] += lax.dot_general(
                tokens[level, :, some], hidden_grad[...], TN, preferred_element_type=f32
            )
        router_grad_ref[...] += lax.dot_general(tokens[level], logit_grad[...], TN, preferred_element_type=f32)

    def order(i):
        return nearest(place, jnp.where(i == 0, 0, jnp.where(i == planes - 1, 1, i + 1)))

    def step(i, carry):
        level, before = order(i), order(i - 1)

        def half(s, carry):
            r = jnp.where(i == 0, s, 1 - s)

            @pl.when((i == 0) & (s == 0))
            def _():
                grads_load(z).wait()
                c_copy(z, 0).wait_recv()

            @pl.when((i == 0) & (s == 1))
            def _():
                hop(1)

            @pl.when((i == 0) == (s == 1))
            def _():
                x_copy(level).wait_recv()
                c_copy(level, 1).start()
                c_copy(level, 1).wait_recv()

            @pl.when((i > 0) & (s == 0))
            def _():
                grads_load(level).wait()

            @pl.when((i > 0) & (s == 1))
            def _():
                @pl.when(i + 2 < planes)
                def _():
                    hop(i + 2)

                level_sum(before)

                @pl.when(before != z)
                def _():
                    sum_z_copy(before, z).start()

                across_sum(level)
                c_copy(level, 0).wait_recv()

            tiles(level, r)
            sum_c_copy(level, r).start()
            mix_store(level, r).start()
            return carry

        lax.fori_loop(0, 2, half, 0)

        @pl.when((i == 0) & (i + 2 < planes))
        def _():
            hop(2)

        @pl.when(i == planes - 1)
        def _():
            level_sum(level)
            sum_z_copy(level, z).start()

        weight_grads(level)

        @pl.when(i == 0)
        def _():
            across_sum(z)

        return carry

    lax.fori_loop(0, planes, step, 0)
    inner_grad_ref[...] = inner_acc[...].astype(bf16)
    outer_grad_ref[...] = outer_acc[...].astype(bf16)
    total = part[z, 0:rows, :].astype(f32)
    for k in range(1, planes):
        source = lax.rem(z + k, planes)
        sum_z_copy(z, source).wait_recv()
        total = total + from_z[source].astype(f32)
    out_ref[...] = total
    for level in range(planes):
        mix_store(level, 0).wait()
        mix_store(level, 1).wait()
        x_copy(level).wait_send()
        c_copy(level, 0).wait_send()
        c_copy(level, 1).wait_send()
        sum_c_copy(level, 0).wait_send()
        sum_c_copy(level, 1).wait_send()
        sum_x_copy(level).wait_send()

        @pl.when(level != z)
        def _():
            sum_z_copy(level, z).wait_send()

        @pl.when((z >= level) & (z < planes - 1))
        def _():
            up_copy(level).wait_send()

        @pl.when((z <= level) & (z > 0))
        def _():
            down_copy(level).wait_send()


def experts_of_the_plane(planes, own, real, normed, grads, inner, outer, bias, small):
    f32, bf16 = jnp.float32, jnp.bfloat16
    rows = normed.shape[0]
    chunk = 4 * rows
    width, units = inner.shape
    shape = jax.ShapeDtypeStruct
    vmem = pl.BlockSpec(memory_space=pltpu.VMEM)
    anywhere = pl.BlockSpec(memory_space=pl.ANY)
    dma = pltpu.SemaphoreType.DMA
    flops = 12 * planes * chunk * width * units
    return pl.pallas_call(
        functools.partial(expert_kernel, planes, own, rows, real),
        out_shape=[
            shape((planes, chunk, width), bf16),
            shape((rows, width), f32),
            shape((width, units), bf16),
            shape((units, width), bf16),
            shape((8, units), f32),
            shape((width, 128), f32),
        ],
        in_specs=[vmem, anywhere, vmem, anywhere, vmem, vmem],
        out_specs=[anywhere] + [vmem] * 5,
        scratch_shapes=[
            pltpu.VMEM((planes, chunk, width), bf16),
            pltpu.VMEM((planes, chunk, width), bf16),
            pltpu.VMEM((units, width), bf16),
            pltpu.VMEM((units, width), bf16),
            pltpu.VMEM((width, units), bf16),
            pltpu.VMEM((width, 128), bf16),
            pltpu.VMEM((128, width), bf16),
            pltpu.VMEM((planes, chunk, width), bf16),
            pltpu.VMEM((planes, chunk, width), bf16),
            pltpu.VMEM((planes, 2 * rows, width), bf16),
            pltpu.VMEM((planes, rows, width), bf16),
            pltpu.VMEM((planes, rows, width), bf16),
            pltpu.VMEM((chunk, units), bf16),
            pltpu.VMEM((chunk, units), bf16),
            pltpu.VMEM((chunk, 128), bf16),
            pltpu.VMEM((width, units), f32),
            pltpu.VMEM((units, width), f32),
            dma((own,)),
            dma((planes,)),
            dma((planes, 2)),
        ]
        + [dma((2, planes))] * 2
        + [dma((planes,))] * 2
        + [dma((planes, 2))] * 4
        + [dma((planes,))] * 4,
        compiler_params=pltpu.CompilerParams(
            collective_id=1, has_side_effects=True, vmem_limit_bytes=60 * 2**20
        ),
        cost_estimate=pl.CostEstimate(flops=flops, bytes_accessed=40 * 2**20, transcendentals=0),
        name="experts_of_the_plane",
    )(normed, grads, inner, outer, bias, small)


def front_kernel(
    planes,
    heads,
    real,
    tokens_ref,
    mask_ref,
    ids_ref,
    cotangent_ref,
    *refs,
):
    vector_refs, refs = refs[:5], refs[5:]
    (
        router_part_ref,
        outer_bias_ref,
        qkv_part_ref,
    proj_part_ref,
    inner_part_ref,
    small_all,
    w_qkv_out,
    w_proj_out,
    inner_all,
    normed_in_ref,
    qkv_ref,
    attended_ref,
    middle_ref,
    normed_ref,
    grad_ref,
    grads_all,
    wide_ref,
    select_ref,
    keys_ref,
    keep_ref,
    w_qkv_all,
    w_proj_all,
    out_sem,
    up_send,
    up_recv,
    down_send,
    down_recv,
    x_send,
    x_recv,
    c_send,
    c_recv,
    over_send,
    over_recv,
    over_c_send,
    over_c_recv,
    g_z_send,
    g_z_recv,
    g_x_send,
    g_x_recv,
    g_c_send,
    g_c_recv,
    spread_send,
    spread_recv,
    own_sem,
    y_send,
    y_recv,
    ) = refs
    f32, bf16 = jnp.float32, jnp.bfloat16
    place = Place(planes)
    rows, width = wide_ref.shape
    depth = qkv_part_ref.shape[0]
    experts = inner_part_ref.shape[0]
    half = depth // 2
    lanes = inner_part_ref.shape[2] // (2 * planes)
    head_dim = width // heads
    y, c, z, x = place.y, place.c, place.z, place.x
    gathered = [small_all, w_qkv_all, w_proj_all]

    def remote(src, dst, send, recv, device):
        return pltpu.make_async_remote_copy(
            src_ref=src, dst_ref=dst, send_sem=send, recv_sem=recv, device_id=device, device_id_type=MESH
        )

    def block(j, level, across, core, plane):
        start = pl.multiple_of((level * 2 + across) * depth + core * half, 16)
        if j == 0:
            return gathered[j].at[pl.ds(start, half)]
        columns = gathered[j].shape[1] // 2
        return gathered[j].at[pl.ds(start, half), pl.ds(pl.multiple_of(plane * columns, 128), columns)]

    def piece(j, level, across):
        return block(j, level, across, c, y)

    def up_copy(j, level):
        here = piece(j, level, x)
        return remote(here, here, up_send.at[j, level], up_recv.at[j, level], place.at(y, c, z + 1, x))

    def down_copy(j, level):
        here = piece(j, level, x)
        return remote(here, here, down_send.at[j, level], down_recv.at[j, level], place.at(y, c, z - 1, x))

    def x_copy(j, level, across):
        here = piece(j, level, across)
        return remote(here, here, x_send.at[j, level], x_recv.at[j, level], place.other_x())

    def c_copy(j, level, across):
        here = piece(j, level, across)
        at = level * 2 + across
        return remote(here, here, c_send.at[j, at], c_recv.at[j, at], place.other_core())

    def over_copy(j, level, across):
        here = piece(j, level, across)
        at = level * 2 + across
        return remote(here, here, over_send.at[j, at], over_recv.at[j, at], place.other_y())

    def over_c_copy(j, level, across):
        here = block(j, level, across, c, 1 - y)
        at = level * 2 + across
        return remote(here, here, over_c_send.at[j, at], over_c_recv.at[j, at], place.other_core())

    def g_slot(level, at):
        return grads_all.at[level, pl.ds(at * rows, rows)]

    def g_up(level):
        here = g_slot(level, 0)
        return remote(here, here, g_z_send.at[0, level], g_z_recv.at[0, level], place.at(y, c, z + 1, x))

    def g_down(level):
        here = g_slot(level, 0)
        return remote(here, here, g_z_send.at[1, level], g_z_recv.at[1, level], place.at(y, c, z - 1, x))

    def g_x(level):
        return remote(g_slot(level, 0), g_slot(level, 2), g_x_send.at[level], g_x_recv.at[level], place.other_x())

    def g_c(level, r):
        return remote(
            g_slot(level, 2 * r), g_slot(level, 2 * r + 1), g_c_send.at[level, r], g_c_recv.at[level, r], place.other_core()
        )

    def columns_of(f):
        return pl.ds(pl.multiple_of(f * lanes, 128), lanes)

    here_rows = pl.ds(pl.multiple_of((z * 2 + x) * depth, 16), depth)
    my_units = pl.ds(pl.multiple_of(y * lanes, 128), lanes)

    def spread_copy(k, r):
        level, across = lax.rem(z + k, planes), (x + r) % 2
        return remote(
            inner_part_ref.at[c * 2 + y, :, columns_of(level * 2 + across)],
            inner_all.at[here_rows, my_units],
            spread_send.at[k, r],
            spread_recv.at[k, r],
            place.at(y, c, level, across),
        )

    own_copy = pltpu.make_async_copy(
        inner_part_ref.at[c * 2 + y, :, columns_of(z * 2 + x)], inner_all.at[here_rows, my_units], own_sem
    )
    y_copy = remote(inner_all.at[:, my_units], inner_all.at[:, my_units], y_send, y_recv, place.other_y())
    their_units = pl.ds(pl.multiple_of((1 - y) * lanes, 128), lanes)
    from_y = remote(inner_all.at[:, their_units], inner_all.at[:, their_units], y_send, y_recv, place.other_y())

    others = [(k, r) for k in range(planes) for r in range(2) if k or r]
    partners = [place.other_core(), place.other_y()]
    partners += [place.at(y, c, lax.rem(z + k, planes), (x + r) % 2) for k, r in others]
    greet(partners)

    w_qkv_all[here_rows, :] = qkv_part_ref[...]

    def share(j, level, across):
        c_copy(j, level, across).start()
        if j:
            over_copy(j, level, across).start()

    def line(flows):
        @pl.when(z < planes - 1)
        def _():
            for j in flows:
                up_copy(j, z).start()

        @pl.when(z > 0)
        def _():
            for j in flows:
                down_copy(j, z).start()

        for j in flows:
            x_copy(j, z, x).start()

    def hops(flows):
        for h in range(1, planes):
            @pl.when(z >= h)
            def _():
                for j in flows:
                    up_copy(j, z - h).wait_recv()

                    @pl.when(z < planes - 1)
                    def _():
                        up_copy(j, z - h).start()

                    x_copy(j, z - h, x).start()
                    share(j, z - h, x)

            @pl.when(z + h < planes)
            def _():
                for j in flows:
                    down_copy(j, z + h).wait_recv()

                    @pl.when(z > 0)
                    def _():
                        down_copy(j, z + h).start()

                    x_copy(j, z + h, x).start()
                    share(j, z + h, x)

    def arrive(flows):
        for i in range(planes):
            level = nearest(place, i)
            for j in flows:
                x_copy(j, level, 1 - x).wait_recv()
                share(j, level, 1 - x)

    def over_arrive(flows):
        for i in range(planes):
            level = nearest(place, i)
            for j in flows:
                if i:
                    over_copy(j, level, x).wait_recv()
                    over_c_copy(j, level, x).start()
                over_copy(j, level, 1 - x).wait_recv()
                over_c_copy(j, level, 1 - x).start()

    def gather_done(flows):
        for level in range(planes):
            for j in flows:
                c_copy(j, level, 1 - x).wait_recv()
                if j:
                    over_c_copy(j, level, 1 - x).wait_recv()

            @pl.when(level != z)
            def _():
                for j in flows:
                    c_copy(j, level, x).wait_recv()
                    if j:
                        over_c_copy(j, level, x).wait_recv()

    def g_hop(h):
        @pl.when(z >= h)
        def _():
            g_up(z - h).wait_recv()

            @pl.when(z < planes - 1)
            def _():
                g_up(z - h).start()

            g_x(z - h).start()
            g_c(z - h, 0).start()

        @pl.when(z + h < planes)
        def _():
            g_down(z + h).wait_recv()

            @pl.when(z > 0)
            def _():
                g_down(z + h).start()

            g_x(z + h).start()
            g_c(z + h, 0).start()

    line([1])
    lined = [ref[...].astype(f32) for ref in vector_refs] + [outer_bias_ref[...].astype(f32)]
    lined = jnp.concatenate(lined, axis=0)
    lined = jnp.concatenate([lined, jnp.zeros((128 - lined.shape[0], depth), f32)], axis=0)
    lined = jnp.concatenate([lined, jnp.zeros((128, 128 - depth), f32)], axis=1)
    routed = jnp.concatenate([router_part_ref[...].astype(f32), jnp.zeros((depth, 128 - experts), f32)], axis=1)
    small = jnp.transpose(lined)[:depth] + pltpu.roll(routed, 5 + experts, 1)
    small_all[here_rows, :] = small.astype(bf16)
    line([0])
    w_proj_all[here_rows, :] = proj_part_ref[...]
    line([2])
    spare = jnp.zeros((rows - real, width), f32)
    values = jnp.concatenate([tokens_ref[...].astype(f32), spare], axis=0)
    wide_ref[...] = values.astype(bf16)
    normal, _ = norm_parts(values)
    mask = mask_ref[pl.ds(y * 2 + c, 1), :].astype(f32)
    keys = jnp.concatenate([mask, jnp.zeros((1, rows - real), f32)], axis=1)
    keys_ref[...] = keys
    keep = lax.broadcasted_iota(jnp.int32, (rows, rows), 0) == lax.broadcasted_iota(jnp.int32, (rows, rows), 1)
    keep = jnp.sum(jnp.where(keep, keys, 0.0), axis=1, keepdims=True)
    keep_ref[...] = keep
    ids = ids_ref[...]
    number = lax.broadcasted_iota(jnp.int32, (real, 128), 1)
    select = ((number == ids[:, 0:1]) | (number == ids[:, 1:2])).astype(f32)
    select = jnp.concatenate([select, jnp.zeros((rows - real, 128), f32)], axis=0)
    select_ref[...] = select.astype(bf16)
    chosen = jnp.transpose(jnp.concatenate([select, jnp.zeros((256 - rows, 128), f32)], axis=0))[:8]
    chosen = jnp.concatenate([chosen, jnp.zeros((8, width - 256), f32)], axis=1)
    if rows - real > 8:
        chosen = jnp.concatenate([chosen, jnp.zeros((rows - real - 8, width), f32)], axis=0)
    grad_out = cotangent_ref[...].astype(f32) * keep[:real]
    grad_out = jnp.concatenate([grad_out, chosen], axis=0).astype(bf16)
    grad_ref[...] = grad_out
    grads_own = pltpu.make_async_copy(grad_ref, g_slot(z, 0), out_sem.at[2])
    grads_own.start()
    hops([1, 0])
    arrive([1, 0])
    hops([2])
    own_copy.start()
    for k, r in others:
        spread_copy(k, r).start()

    grads_own.wait()

    @pl.when(z < planes - 1)
    def _():
        g_up(z).start()

    @pl.when(z > 0)
    def _():
        g_down(z).start()

    g_x(z).start()
    g_c(z, 0).start()
    arrive([2])
    over_arrive([1])
    gather_done([1, 0])
    qkv_out_copy = pltpu.make_async_copy(w_qkv_all, w_qkv_out, out_sem.at[0])
    qkv_out_copy.start()
    vectors = jnp.transpose(small_all[...].astype(f32))
    normed_in = (normal * vectors[0:1] + vectors[1:2]).astype(bf16)
    normed_in_ref[...] = normed_in
    for j in range(3):
        part = slice(j * width, (j + 1) * width)
        qkv_ref[:, part] = dot(normed_in, w_qkv_all[:, part]).astype(bf16)
    g_hop(1)
    over_arrive([2])
    lane = lax.broadcasted_iota(jnp.int32, (rows, 2 * head_dim), 1)
    usable = keys_ref[...] > 0
    for pair in range(heads // 2):
        if pair == heads // 4:
            g_hop(2)
        at = pair * 2 * head_dim
        queries = qkv_ref[:, at : at + 2 * head_dim]
        keys = qkv_ref[:, width + at : width + at + 2 * head_dim]
        held = qkv_ref[:, 2 * width + at : 2 * width + at + 2 * head_dim]
        outs = []
        for side in range(2):
            only = (lane < head_dim) if side == 0 else (lane >= head_dim)
            scores = lax.dot_general(
                jnp.where(only, queries, 0).astype(bf16), keys, NT, preferred_element_type=f32
            )
            scores = jnp.where(usable, scores * head_dim ** (-0.5), masked_score)
            shifted = jnp.exp(scores - jnp.max(scores, axis=1, keepdims=True))
            probs = (shifted / jnp.sum(shifted, axis=1, keepdims=True)).astype(bf16)
            outs.append(dot(probs, held))
        attended_ref[:, at : at + 2 * head_dim] = jnp.where(lane < head_dim, outs[0], outs[1]).astype(bf16)
    for h in range(3, planes):
        g_hop(h)
    own_copy.wait()
    for k, r in others:
        spread_copy(k, r).wait_recv()
    y_copy.start()
    gather_done([2])
    proj_out_copy = pltpu.make_async_copy(w_proj_all, w_proj_out, out_sem.at[1])
    proj_out_copy.start()
    middle = values + dot(attended_ref[...], w_proj_all[...]) + vectors[2:3]
    middle_ref[...] = middle
    normal_mid, _ = norm_parts(middle)
    normed = normal_mid * vectors[3:4] + vectors[4:5]
    row = lax.broadcasted_iota(jnp.int32, normed.shape, 0)
    normed_ref[...] = jnp.where(row < real, normed, 0.0).astype(bf16)
    for i in range(planes):
        level = nearest(place, i)
        g_x(level).wait_recv()
        g_c(level, 1).start()
    from_y.wait_recv()
    qkv_out_copy.wait()
    proj_out_copy.wait()
    for level in range(planes):
        g_c(level, 0).wait_recv()
        g_c(level, 1).wait_recv()
    y_copy.wait_send()
    for k, r in others:
        spread_copy(k, r).wait_send()
    for level in range(planes):
        g_x(level).wait_send()
        g_c(level, 0).wait_send()
        g_c(level, 1).wait_send()

        @pl.when((z >= level) & (z < planes - 1))
        def _():
            g_up(level).wait_send()

        @pl.when((z <= level) & (z > 0))
        def _():
            g_down(level).wait_send()

    def shared(j, level, across):
        c_copy(j, level, across).wait_send()
        if j:
            over_copy(j, level, across).wait_send()
            over_c_copy(j, level, across).wait_send()

    for j in range(3):
        for level in range(planes):
            x_copy(j, level, x).wait_send()
            shared(j, level, 1 - x)

            @pl.when(level != z)
            def _():
                shared(j, level, x)

            @pl.when((z >= level) & (z < planes - 1))
            def _():
                up_copy(j, level).wait_send()

            @pl.when((z <= level) & (z > 0))
            def _():
                down_copy(j, level).wait_send()


def front(planes, rows, tokens, mask, ids, cotangent, vectors, router, outer_bias, w_qkv, w_proj, w_in):
    f32, bf16 = jnp.float32, jnp.bfloat16
    real, width = tokens.shape
    lanes = w_in.shape[2] // (2 * planes)
    shape = jax.ShapeDtypeStruct
    vmem = pl.BlockSpec(memory_space=pltpu.VMEM)
    anywhere = pl.BlockSpec(memory_space=pl.ANY)
    dma = pltpu.SemaphoreType.DMA
    return pl.pallas_call(
        functools.partial(front_kernel, planes, HEADS, real),
        out_shape=[
            shape((width, 128), bf16),
            shape((width, 3 * width), bf16),
            shape((width, width), bf16),
            shape((width, 2 * lanes), bf16),
            shape((rows, width), bf16),
            shape((rows, 3 * width), bf16),
            shape((rows, width), bf16),
            shape((rows, width), f32),
            shape((rows, width), bf16),
            shape((rows, width), bf16),
            shape((planes, 4 * rows, width), bf16),
            shape((rows, width), bf16),
            shape((rows, 128), bf16),
            shape((1, rows), f32),
            shape((rows, 1), f32),
        ],
        in_specs=[vmem] * (6 + len(vectors)) + [vmem] * 2 + [anywhere],
        out_specs=[vmem] + [anywhere] * 3 + [vmem] * 6 + [anywhere] + [vmem] * 4,
        scratch_shapes=[pltpu.VMEM((width, 3 * width), bf16), pltpu.VMEM((width, width), bf16), dma((3,))]
        + [dma((3, planes))] * 6
        + [dma((3, 2 * planes))] * 6
        + [dma((2, planes))] * 2
        + [dma((planes,))] * 2
        + [dma((planes, 2))] * 4
        + [dma] * 3,
        compiler_params=pltpu.CompilerParams(
            collective_id=2, has_side_effects=True, vmem_limit_bytes=60 * 2**20
        ),
        cost_estimate=pl.CostEstimate(flops=2**32, bytes_accessed=40 * 2**20, transcendentals=0),
        name="dense_weights_and_attention",
    )(tokens, mask, ids, cotangent, *vectors, router, outer_bias, w_qkv, w_proj, w_in)


def back_kernel(planes, heads, own, groups, real, *refs):
    (
        row_grad_ref,
        normed_ref,
        grad_ref,
        middle_ref,
        tokens_ref,
        normed_in_ref,
        qkv_ref,
        attended_ref,
        small_ref,
        w_qkv_all_ref,
        w_proj_ref,
        keys_ref,
        keep_ref,
        select_ref,
        mix_ref,
        inner_ref,
        outer_ref,
        bias_ref,
        router_grad_ref,
    ) = refs[:19]
    mixed_ref, token_grad_ref, qkv_out, proj_out, small_out, inner_out, outer_out, bias_out = refs[19:27]
    refs = refs[27:]
    (
        w_qkv_ref,
        outer_sum,
        grad_attended,
        grad_qkv,
        mix_x,
        mix_z,
        mix_from_core,
        mix_from_x,
        mix_from_z,
        inner_from_y,
        inner_sum,
        outer_from_y,
        bias_from_y,
        held,
        held_small,
        from_core,
        from_core_small,
        from_x,
        from_x_small,
        from_z,
        from_z_small,
        plane_sum,
        plane_sum_small,
        from_y,
        from_y_small,
        final,
        final_small,
    ) = refs[:27]
    (
        load_sem,
        outer_own_sem,
        mix_c_send,
        mix_c_recv,
        mix_x_send,
        mix_x_recv,
        mix_z_send,
        mix_z_recv,
        inner_y_sem,
        spread_send,
        spread_recv,
        inner_back_sem,
        inner_core_sem,
        outer_y_sem,
        outer_c_sem,
        bias_y_sem,
        bias_c_sem,
        own_sem,
        flow_c_sem,
        flow_x_sem,
        flow_z_send,
        flow_z_recv,
        flow_y_sem,
        flow_end_sem,
    ) = refs[27:]
    f32, bf16 = jnp.float32, jnp.bfloat16
    place = Place(planes)
    y, c, z, x = place.y, place.c, place.z, place.x
    rows, width = middle_ref.shape
    depth = width // (2 * planes)
    half = depth // 2
    lanes = inner_ref.shape[1] // own
    head_dim = width // heads
    pair_width = 2 * head_dim
    small_at = groups + 1

    def remote(src, dst, send, recv, device):
        return pltpu.make_async_remote_copy(
            src_ref=src, dst_ref=dst, send_sem=send, recv_sem=recv, device_id=device, device_id_type=MESH
        )

    def swap(src, dst, sem, device):
        return remote(src, dst, sem.at[0], sem.at[1], device)

    def of_flow(j, many, alone):
        return alone if j == small_at else many.at[j]

    mine, theirs = pl.ds(pl.multiple_of(c * half, 16), half), pl.ds(pl.multiple_of((1 - c) * half, 16), half)

    def flow_c(j):
        source = of_flow(j, held, held_small)
        return swap(
            source.at[:, :, theirs], of_flow(j, from_core, from_core_small), flow_c_sem.at[j], place.other_core()
        )

    def flow_x(j):
        source = of_flow(j, held, held_small)
        return swap(source.at[:, 1 - x, mine], of_flow(j, from_x, from_x_small), flow_x_sem.at[j], place.other_x())

    def flow_z(j, k):
        level = lax.rem(z + k, planes)
        source = of_flow(j, held, held_small)
        return remote(
            source.at[level, x, mine],
            of_flow(j, from_z, from_z_small).at[k],
            flow_z_send.at[j, k],
            flow_z_recv.at[j, k],
            place.level(k),
        )

    def flow_y(j):
        return swap(
            of_flow(j, plane_sum, plane_sum_small),
            of_flow(j, from_y, from_y_small),
            flow_y_sem.at[j],
            place.other_y(),
        )

    def flow_end(j):
        here = of_flow(j, final, final_small).at[mine]
        return swap(here, here, flow_end_sem.at[j], place.other_core())

    def flow_core_sum(j):
        flow_c(j).wait_recv()
        kept = of_flow(j, held, held_small)
        total = kept[:, :, mine, :].astype(f32) + of_flow(j, from_core, from_core_small)[...].astype(f32)
        kept[:, :, mine, :] = total.astype(bf16)
        flow_x(j).start()

    def flow_x_sum(j):
        flow_x(j).wait_recv()
        kept = of_flow(j, held, held_small)
        total = kept[:, x, mine, :].astype(f32) + of_flow(j, from_x, from_x_small)[...].astype(f32)
        kept[:, x, mine, :] = total.astype(bf16)
        for k in range(1, planes):
            flow_z(j, k).start()

    def flow_z_sum(j):
        kept = of_flow(j, held, held_small)
        total = kept[z, x, mine, :].astype(f32)
        for k in range(1, planes):
            flow_z(j, k).wait_recv()
            total = total + of_flow(j, from_z, from_z_small)[k].astype(f32)
        of_flow(j, plane_sum, plane_sum_small)[...] = total.astype(bf16)
        flow_y(j).start()

    def flow_y_sum(j):
        flow_y(j).wait_recv()
        total = of_flow(j, plane_sum, plane_sum_small)[...].astype(f32)
        total = total + of_flow(j, from_y, from_y_small)[...].astype(f32)
        of_flow(j, final, final_small)[mine, :] = total.astype(bf16)
        flow_end(j).start()

    loads = [
        pltpu.make_async_copy(mix_ref.at[:, pl.ds(2 * rows, rows)], mix_x, load_sem.at[0]),
        pltpu.make_async_copy(mix_ref.at[:, pl.ds(0, rows)], mix_z, load_sem.at[1]),
        pltpu.make_async_copy(w_qkv_all_ref, w_qkv_ref, load_sem.at[2]),
    ]

    def mix_c(r):
        return remote(
            mix_ref.at[:, pl.ds((2 * r + 1) * rows, rows)],
            mix_from_core.at[:, pl.ds(r * rows, rows)],
            mix_c_send.at[r],
            mix_c_recv.at[r],
            place.other_core(),
        )

    def mix_to_x(level):
        return remote(mix_x.at[level], mix_from_x.at[level], mix_x_send.at[level], mix_x_recv.at[level], place.other_x())

    def mix_to_z(level, source):
        return remote(
            mix_z.at[level], mix_from_z.at[source], mix_z_send.at[level], mix_z_recv.at[source], place.at(y, c, level, x)
        )

    def mix_core_sum():
        for load in loads[:2]:
            load.wait()
        mix_c(0).wait_recv()
        mix_c(1).wait_recv()
        for k in range(1, planes + 1):
            level = lax.rem(z + k, planes)
            total = mix_x[level].astype(f32) + mix_from_core[level, rows:, :].astype(f32)
            mix_x[level] = total.astype(bf16)
            mix_to_x(level).start()
        for level in range(planes):
            total = mix_z[level].astype(f32) + mix_from_core[level, :rows, :].astype(f32)
            mix_z[level] = total.astype(bf16)

    def mix_x_sum(k):
        level = lax.rem(z + k, planes)
        mix_to_x(level).wait_recv()
        mix_z[level] = (mix_z[level].astype(f32) + mix_from_x[level].astype(f32)).astype(bf16)
        if k < planes:
            mix_to_z(level, z).start()

    my_units = pl.ds(pl.multiple_of(y * lanes, 128), lanes)
    their_units = pl.ds(pl.multiple_of((1 - y) * lanes, 128), lanes)
    my_expert, their_expert = c * 2 + y, c * 2 + 1 - y
    my_columns = pl.ds(pl.multiple_of((z * 2 + x) * lanes, 128), lanes)

    def inner_y():
        return swap(inner_ref.at[:, their_units], inner_from_y, inner_y_sem, place.other_y())

    def shard_rows(f):
        return pl.ds(pl.multiple_of(f * depth, 16), depth)

    def spread(k, r):
        level, across = lax.rem(z + k, planes), (x + r) % 2
        return remote(
            inner_sum.at[shard_rows(level * 2 + across)],
            inner_out.at[my_expert, :, my_columns],
            spread_send.at[k, r],
            spread_recv.at[k, r],
            place.at(y, c, level, across),
        )

    own_copy = pltpu.make_async_copy(
        inner_sum.at[shard_rows(z * 2 + x)], inner_out.at[my_expert, :, my_columns], own_sem
    )

    def inner_back():
        here = inner_out.at[my_expert]
        return swap(here, here, inner_back_sem, place.other_y())

    def inner_core(expert, at):
        here = inner_out.at[expert]
        return swap(here, here, inner_core_sem.at[at], place.other_core())

    def outer_y():
        return swap(outer_ref, outer_from_y, outer_y_sem, place.other_y())

    def outer_c():
        return swap(outer_sum, outer_out.at[c], outer_c_sem, place.other_core())

    outer_own = pltpu.make_async_copy(outer_sum, outer_out.at[c], outer_own_sem)

    def bias_y():
        return swap(bias_ref, bias_from_y, bias_y_sem, place.other_y())

    def bias_c():
        here = bias_out.at[c]
        return swap(here, here, bias_c_sem, place.other_core())

    others = [(k, r) for k in range(planes) for r in range(2) if k or r]

    def inner_y_sum():
        inner_y().wait_recv()
        total = inner_ref[:, my_units].astype(f32) + inner_from_y[...].astype(f32)
        inner_sum[...] = total.astype(bf16)
        own_copy.start()
        for k, r in others:
            spread(k, r).start()
        outer_y().start()

    def inner_spread_done():
        own_copy.wait()
        for k, r in others:
            spread(k, r).wait_recv()
        inner_back().start()
        inner_core(my_expert, 0).start()

    def outer_y_sum():
        outer_y().wait_recv()
        total = outer_ref[...].astype(f32) + outer_from_y[...].astype(f32)
        outer_sum[...] = total.astype(bf16)
        outer_own.start()
        outer_c().start()
        bias_y().wait_recv()
        bias_out[c] = bias_ref[...] + bias_from_y[...]
        bias_c().start()

    partners = [place.other_core(), place.other_y()]
    partners += [place.at(y, c, lax.rem(z + k, planes), (x + r) % 2) for k, r in others]
    greet(partners)
    inner_y().start()
    bias_y().start()
    mix_c(1).start()
    mix_c(0).start()
    for load in loads:
        load.start()

    vectors = jnp.transpose(small_ref[...].astype(f32))
    gain_first, gain_second = vectors[0:1], vectors[3:4]
    place_row = lax.broadcasted_iota(jnp.int32, (128, 128), 0)
    place_lane = lax.broadcasted_iota(jnp.int32, (128, 128), 1)

    def lanes_from(first):
        take = (place_row == place_lane + first) & (place_lane < 2 * own)
        return dot(small_ref[...], take.astype(bf16)).astype(bf16)

    outer_bias, router = lanes_from(5), lanes_from(5 + 2 * own)
    normed_mid, grad_out = normed_ref[...], grad_ref[...]
    real_row = lax.broadcasted_iota(jnp.int32, grad_out.shape, 0) < real
    grad_out = jnp.where(real_row, grad_out, 0).astype(bf16)
    select = select_ref[...].astype(f32)
    lane = lax.broadcasted_iota(jnp.int32, select.shape, 1)
    logits = jnp.where(lane < 2 * own, dot(normed_mid, router), -1e30)
    routing = jnp.exp(logits - jnp.max(logits, axis=1, keepdims=True))
    routing = routing / jnp.sum(routing, axis=1, keepdims=True)
    gates = routing * select
    bias_gate = select * dot(grad_out, outer_bias)
    bias_logits = routing * (bias_gate - jnp.sum(routing * bias_gate, axis=1, keepdims=True))
    bias_logits = bias_logits.astype(bf16)
    router_grad = lax.dot_general(normed_mid, bias_logits, TN, preferred_element_type=f32)
    router_grad = pltpu.roll(router_grad, 16, 1) + pltpu.roll(router_grad_ref[...], 16 - real % 16, 1)
    outer_bias_grad = lax.dot_general(gates.astype(bf16), grad_out, TN, preferred_element_type=f32)
    grad_normed_mid = row_grad_ref[...] + lax.dot_general(bias_logits, router, NT, preferred_element_type=f32)
    normal_mid, rstd_mid = norm_parts(middle_ref[...])
    gain_second_grad = jnp.sum(grad_normed_mid * normal_mid, axis=0, keepdims=True)
    bias_second_grad = jnp.sum(grad_normed_mid, axis=0, keepdims=True)
    grad_middle = grad_out.astype(f32) + norm_back(grad_normed_mid, normal_mid, rstd_mid, gain_second)
    grad_proj = grad_middle.astype(bf16)
    proj_bias_grad = jnp.sum(grad_proj.astype(f32), axis=0, keepdims=True)
    mix_core_sum()

    def hold(j, value):
        held[j] = value.astype(bf16).reshape(planes, 2, depth, width)
        flow_c(j).start()

    hold(0, lax.dot_general(attended_ref[...], grad_proj, TN, preferred_element_type=f32))
    grad_attended[...] = lax.dot_general(grad_proj, w_proj_ref[...], NT, preferred_element_type=f32).astype(bf16)
    flow_core_sum(0)

    pair_lane = lax.broadcasted_iota(jnp.int32, (rows, pair_width), 1)
    usable = keys_ref[...] > 0
    scaling = head_dim ** (-0.5)
    group_width = width // groups

    def pair_back(pair):
        at = pair * pair_width
        group, inside = at // group_width, at % group_width
        queries = qkv_ref[:, at : at + pair_width]
        keys = qkv_ref[:, width + at : width + at + pair_width]
        values = qkv_ref[:, 2 * width + at : 2 * width + at + pair_width]
        grads = grad_attended[:, at : at + pair_width]
        found = []
        for side in range(2):
            only = (pair_lane < head_dim) if side == 0 else (pair_lane >= head_dim)
            some_queries = jnp.where(only, queries, 0).astype(bf16)
            some_grads = jnp.where(only, grads, 0).astype(bf16)
            scores = lax.dot_general(some_queries, keys, NT, preferred_element_type=f32)
            scores = jnp.where(usable, scores * scaling, masked_score)
            shifted = jnp.exp(scores - jnp.max(scores, axis=1, keepdims=True))
            probs = shifted / jnp.sum(shifted, axis=1, keepdims=True)
            grad_probs = lax.dot_general(some_grads, values, NT, preferred_element_type=f32)
            grad_scores = probs * (grad_probs - jnp.sum(probs * grad_probs, axis=1, keepdims=True))
            grad_scores = grad_scores.astype(bf16)
            found.append(
                (
                    dot(grad_scores, keys),
                    lax.dot_general(grad_scores, some_queries, TN, preferred_element_type=f32),
                    lax.dot_general(probs.astype(bf16), some_grads, TN, preferred_element_type=f32),
                )
            )
        grad_queries = jnp.where(pair_lane < head_dim, found[0][0], found[1][0]) * scaling
        grad_keys = (found[0][1] + found[1][1]) * scaling
        grad_values = found[0][2] + found[1][2]
        for part, value in enumerate((grad_queries, grad_keys, grad_values)):
            start = part * group_width + inside
            grad_qkv[group, :, start : start + pair_width] = value.astype(bf16)

    def group_back(group):
        per_group = heads // 2 // groups
        for pair in range(group * per_group, (group + 1) * per_group):
            pair_back(pair)
        hold(
            1 + group,
            lax.dot_general(normed_in_ref[...], grad_qkv[group], TN, preferred_element_type=f32),
        )

    group_back(0)
    inner_y_sum()
    flow_core_sum(1)
    mix_x_sum(1)
    for group in range(1, groups):
        group_back(group)
        flow_core_sum(1 + group)
        if group == 1:
            mix_x_sum(2)

    loads[2].wait()
    grad_normed_in = jnp.zeros((rows, width), f32)
    for group in range(groups):
        for part in range(3):
            grad_normed_in = grad_normed_in + lax.dot_general(
                grad_qkv[group, :, part * group_width : (part + 1) * group_width],
                w_qkv_ref[:, part * width + group * group_width : part * width + (group + 1) * group_width],
                NT,
                preferred_element_type=f32,
            )
    normal_first, rstd_first = norm_parts(tokens_ref[...].astype(f32))
    gain_first_grad = jnp.sum(grad_normed_in * normal_first, axis=0, keepdims=True)
    bias_first_grad = jnp.sum(grad_normed_in, axis=0, keepdims=True)
    token_grad = grad_middle + norm_back(grad_normed_in, normal_first, rstd_first, gain_first)
    token_grad_ref[...] = token_grad.astype(bf16)[:real]
    vector_rows = jnp.concatenate(
        [
            gain_first_grad,
            bias_first_grad,
            proj_bias_grad,
            gain_second_grad,
            bias_second_grad,
            jnp.zeros((3, width), f32),
            outer_bias_grad[:8],
            jnp.zeros((112, width), f32),
        ],
        axis=0,
    )
    vector_grads = jnp.transpose(vector_rows) + router_grad
    held_small[...] = vector_grads.astype(bf16).reshape(planes, 2, depth, 128)
    flow_c(small_at).start()
    flow_core_sum(small_at)
    for k in range(3, planes):
        mix_x_sum(k)
    inner_spread_done()
    flow_x_sum(0)
    flow_x_sum(1)
    mix_x_sum(planes)
    outer_y_sum()
    for group in range(1, groups):
        flow_x_sum(1 + group)
    flow_z_sum(0)
    flow_x_sum(small_at)
    mixture = mix_z[z].astype(f32) + dot(gates.astype(bf16), jnp.transpose(outer_bias.astype(f32)).astype(bf16))
    for k in range(1, planes):
        source = lax.rem(z + k, planes)
        mix_to_z(z, source).wait_recv()
        mixture = mixture + mix_from_z[source].astype(f32)
    mixed = (keep_ref[...] * (middle_ref[...] + mixture)).astype(bf16)
    mixed_ref[...] = mixed[:real]
    flow_y_sum(0)
    for group in range(groups):
        flow_z_sum(1 + group)
    flow_z_sum(small_at)
    inner_back().wait_recv()
    inner_core(their_expert, 1).start()
    for group in range(groups):
        flow_y_sum(1 + group)
    flow_y_sum(small_at)

    def arrived(j):
        here = of_flow(j, final, final_small).at[theirs]
        swap(here, here, flow_end_sem.at[j], place.other_core()).wait_recv()

    arrived(0)
    proj_out[...] = final[0]
    for group in range(groups):
        arrived(1 + group)
        for part in range(3):
            start = part * width + group * group_width
            qkv_out[:, start : start + group_width] = final[
                1 + group, :, part * group_width : (part + 1) * group_width
            ]
    arrived(small_at)
    small_out[...] = final_small[...].astype(f32)
    outer_own.wait()
    outer_c().wait_recv()
    bias_theirs = bias_out.at[1 - c]
    swap(bias_theirs, bias_theirs, bias_c_sem, place.other_core()).wait_recv()
    for at, expert in enumerate(((1 - c) * 2 + y, (1 - c) * 2 + 1 - y)):
        inner_core(expert, at).wait_recv()

    mix_c(0).wait_send()
    mix_c(1).wait_send()
    inner_y().wait_send()
    inner_back().wait_send()
    inner_core(my_expert, 0).wait_send()
    inner_core(their_expert, 1).wait_send()
    outer_y().wait_send()
    outer_c().wait_send()
    bias_y().wait_send()
    bias_c().wait_send()
    for k, r in others:
        spread(k, r).wait_send()
    for k in range(1, planes + 1):
        level = lax.rem(z + k, planes)
        mix_to_x(level).wait_send()
        if k < planes:
            mix_to_z(level, z).wait_send()
    for j in range(groups + 2):
        flow_c(j).wait_send()
        flow_x(j).wait_send()
        for k in range(1, planes):
            flow_z(j, k).wait_send()
        flow_y(j).wait_send()
        flow_end(j).wait_send()


def back(planes, own, real, *args):
    f32, bf16 = jnp.float32, jnp.bfloat16
    (
        row_grad,
        normed_mid,
        grad_out,
        middle,
        tokens,
        normed_in,
        qkv,
        attended,
        small,
        w_qkv,
        w_proj,
        keys,
        keep,
        select,
        mix_parts,
        inner_grad,
        outer_grad,
        bias_grad,
        router_grad,
    ) = args
    rows, width = middle.shape
    depth = width // (2 * planes)
    half = depth // 2
    lanes = inner_grad.shape[1] // own
    tall = outer_grad.shape[0]
    pairs = HEADS // 2
    groups = 3 if pairs % 3 == 0 and (pairs // 3) * 2 * (width // HEADS) % 128 == 0 else 1
    flows = groups + 1
    shape = jax.ShapeDtypeStruct
    vmem = pl.BlockSpec(memory_space=pltpu.VMEM)
    anywhere = pl.BlockSpec(memory_space=pl.ANY)
    dma = pltpu.SemaphoreType.DMA

    def both(*dims):
        return [pltpu.VMEM((flows, *dims, width), bf16), pltpu.VMEM((*dims, 128), bf16)]

    return pl.pallas_call(
        functools.partial(back_kernel, planes, HEADS, own, groups, real),
        out_shape=[
            shape((real, width), bf16),
            shape((real, width), bf16),
            shape((depth, 3 * width), bf16),
            shape((depth, width), bf16),
            shape((depth, 128), f32),
            shape((2 * own, depth, 2 * planes * lanes), bf16),
            shape((2, tall, width), bf16),
            shape((2, *bias_grad.shape), f32),
        ],
        in_specs=[vmem] * 9 + [anywhere] + [vmem] * 4 + [anywhere] + [vmem] * 4,
        out_specs=[vmem] * 5 + [anywhere] * 2 + [vmem],
        scratch_shapes=[
            pltpu.VMEM((width, 3 * width), bf16),
            pltpu.VMEM((tall, width), bf16),
            pltpu.VMEM((rows, width), bf16),
            pltpu.VMEM((groups, rows, 3 * width // groups), bf16),
            pltpu.VMEM((planes, rows, width), bf16),
            pltpu.VMEM((planes, rows, width), bf16),
            pltpu.VMEM((planes, 2 * rows, width), bf16),
            pltpu.VMEM((planes, rows, width), bf16),
            pltpu.VMEM((planes, rows, width), bf16),
            pltpu.VMEM((width, lanes), bf16),
            pltpu.VMEM((width, lanes), bf16),
            pltpu.VMEM((tall, width), bf16),
            pltpu.VMEM(bias_grad.shape, f32),
        ]
        + both(planes, 2, depth)
        + both(planes, 2, half)
        + both(planes, half)
        + both(planes, half)
        + both(half)
        + both(half)
        + both(depth)
        + [dma((3,)), dma]
        + [dma((2,))] * 2
        + [dma((planes,))] * 4
        + [dma((2,))]
        + [dma((planes, 2))] * 2
        + [dma((2,)), dma((2, 2)), dma((2,)), dma((2,)), dma((2,)), dma((2,)), dma]
        + [dma((flows + 1, 2))] * 2
        + [dma((flows + 1, planes))] * 2
        + [dma((flows + 1, 2))] * 2,
        compiler_params=pltpu.CompilerParams(
            collective_id=3, has_side_effects=True, vmem_limit_bytes=60 * 2**20
        ),
        cost_estimate=pl.CostEstimate(flops=2**33, bytes_accessed=40 * 2**20, transcendentals=0),
        name="attention_backward_and_sums",
    )(*args)


def norm_parts(values):
    center = values - jnp.mean(values, axis=-1, keepdims=True)
    rstd = lax.rsqrt(jnp.mean(center * center, axis=-1, keepdims=True) + epsilon)
    return center * rstd, rstd


def norm_back(grad, normal, rstd, gain):
    scaled = grad * gain
    return rstd * (
        scaled
        - jnp.mean(scaled, axis=-1, keepdims=True)
        - normal * jnp.mean(scaled * normal, axis=-1, keepdims=True)
    )


def move_tokens_plan(
    tokens,
    key_mask,
    expert_ids,
    cotangent,
    norm1_gain,
    norm1_bias,
    w_qkv,
    w_proj,
    proj_bias,
    norm2_gain,
    norm2_bias,
    w_router,
    w_in,
    b_in,
    w_out,
    b_out,
):
    f32 = jnp.float32
    _, rows, width = tokens.shape
    experts, depth, hidden = w_in.shape
    slice_width = w_out.shape[1]
    planes = hidden // slice_width // 2
    own = experts // 2
    padded = (rows + experts + 15) // 16 * 16
    vectors = [v[None] for v in (norm1_gain, norm1_bias, proj_bias, norm2_gain, norm2_bias)]
    fronts = front(
        planes,
        padded,
        tokens[0],
        key_mask,
        expert_ids[0],
        cotangent[0],
        vectors,
        w_router,
        b_out,
        w_qkv,
        w_proj,
        w_in,
    )
    small, full_qkv, full_proj, inner, normed_in, qkv, attended, middle = fronts[:8]
    normed_mid, grad_out, all_grad_out, wide, select, keys, keep = fronts[8:]
    mix_parts, row_grad, inner_grad, outer_grad, bias_grad, router_grad = experts_of_the_plane(
        planes, own, rows, normed_mid, all_grad_out, inner, w_out, b_in, small
    )
    mixed, token_grad, qkv_grad, proj_grad, vector_grads, inner_grad, outer_grad, bias_grad = back(
        planes,
        own,
        rows,
        row_grad,
        normed_mid,
        grad_out,
        middle,
        wide,
        normed_in,
        qkv,
        attended,
        small,
        full_qkv,
        full_proj,
        keys,
        keep,
        select,
        mix_parts,
        inner_grad,
        outer_grad,
        bias_grad,
        router_grad,
    )
    return (
        mixed[None],
        token_grad[None],
        vector_grads[:, 0],
        vector_grads[:, 1],
        qkv_grad.astype(f32),
        proj_grad.astype(f32),
        vector_grads[:, 2],
        vector_grads[:, 3],
        vector_grads[:, 4],
        vector_grads[:, 16 : 16 + experts],
        inner_grad.astype(f32),
        bias_grad[:, 0].reshape(experts, slice_width),
        outer_grad.reshape(experts, slice_width, width).astype(f32),
        vector_grads[:, 8 : 8 + experts].T,
    )


def solution(mesh):
    n_seq, n_fsdp = mesh.shape["seq"], mesh.shape["fsdp"]

    def per_device(*args):
        tokens, w_in, w_out = args[0], args[12], args[14]
        experts, _, hidden = w_in.shape
        lanes = hidden // n_fsdp
        whole_tiles = lanes % 128 == 0 and tokens.shape[2] % 256 == 0 and w_in.shape[1] % 32 == 0 and 2 * lanes <= tokens.shape[2]
        if n_seq == 4 and experts == n_seq and tokens.shape[0] == 1 and whole_tiles:
            return move_tokens_plan(*args)
        return gather_weights_plan(*args)

    return jax.shard_map(
        per_device,
        mesh=mesh,
        in_specs=(
            P(("fsdp", "seq"), None, None),
            P("fsdp", None),
            P(("fsdp", "seq"), None, None),
            P(("fsdp", "seq"), None, None),
            P("fsdp"),
            P("fsdp"),
            P("fsdp", None),
            P("fsdp", None),
            P("fsdp"),
            P("fsdp"),
            P("fsdp"),
            P("fsdp", None),
            P(None, "fsdp", None),
            P(None, "fsdp"),
            P(None, "fsdp", None),
            P(None, "fsdp"),
        ),
        out_specs=(
            P(("fsdp", "seq"), None, None),
            P(("fsdp", "seq"), None, None),
            P("fsdp"),
            P("fsdp"),
            P("fsdp", None),
            P("fsdp", None),
            P("fsdp"),
            P("fsdp"),
            P("fsdp"),
            P("fsdp", None),
            P(None, "fsdp", None),
            P(None, "fsdp"),
            P(None, "fsdp", None),
            P(None, "fsdp"),
        ),
        check_vma=False,
    )
```

profile of v0, /device:TPU:0, one launch (start us, length us, event | category | flops | bytes accessed | tf_op | source)
XLA Modules:
  0.0 270.0 jit_solution(17988186138797111803)
XLA Ops:
  0.6 1.4 copy.35.refs_5_
  2.0 1.4 copy.34
  3.5 71.4 %dense_weights_and_attention.1 = (bf16[768,128]{1,0:T(8,128)(2,1)}, bf16[768,2304]{1,0:T(8,128)(2,1)}, bf16[768,768]{1,0:T(8,128)(2,1)}, bf16[768,768]{1,0:T(8,1...) custom-call(bf16[200,768]{1,0:T(8,128)(2,1)} %bitcast.18, ...), custom_call_target="tpu_custom_call" | custom-call | flops 4294967296 | bytes 41943040 | tf_op jit(solution)/shard_map/dense_weights_and_attention/pallas_call | solution.py:1223
  74.9 84.5 %experts_of_the_plane.1 = (bf16[4,832,768]{2,1,0:T(8,128)(2,1)}, f32[208,768]{1,0:T(8,128)}, bf16[768,768]{1,0:T(8,128)(2,1)}, bf16[768,768]{1,0:T(8,128)(2,1)}, f32[8,768]{1,0:T(8,128)}, /*index=5*/f32[768,128]{1,0:T(8,128)}) custom-call(bf16[208,768]{1,0:T(8,128)(2,1)} %get-tuple-element.43.normed_ref.refs_1_, ...), custom_call_target="tpu_custom_call" | custom-call | flops 23555211264 | bytes 41943040 | tf_op jit(solution)/shard_map/experts_of_the_plane/pallas_call | solution.py:757
  159.4 94.6 %attention_backward_and_sums.1 = (bf16[200,768]{1,0:T(8,128)(2,1)}, bf16[200,768]{1,0:T(8,128)(2,1)}, bf16[96,2304]{1,0:T(8,128)(2,1)}, bf16[96,768]{1,0:T(8,128...) custom-call(f32[208,768]{1,0:T(8,128)} %get-tuple-element.47.refs_0_, ...), custom_call_target="tpu_custom_call" | custom-call | flops 8589934592 | bytes 41943040 | tf_op jit(solution)/shard_map/attention_backward_and_sums/pallas_call | solution.py:1802
  254.0 0.0 copy-start.1
  254.0 1.9 slice_reduce_fusion
  255.9 0.8 slice_reduce_fusion.5
  256.7 0.6 reshape_squeeze.3
  257.3 1.0 slice_bitcast_fusion
  258.3 0.7 copy.37
  258.9 0.7 copy.36
  259.6 1.6 convert_element_type.16
  261.2 2.0 convert_element_type.15
  263.2 0.0 copy-done.1
  263.2 0.0 copy-start
  263.2 2.8 %convert_element_type.17 = f32[4,96,3072]{2,1,0:T(8,128)} convert(bf16[4,96,3072]{2,1,0:T(8,128)(2,1)S(1)} %copy-done.1) | non-fusion elementwise | flops 1179648 | bytes 7077888 | tf_op jit(solution)/shard_map/convert_element_type | solution.py:1950
  266.0 0.0 copy-done
  266.0 0.0 copy-start.3
  266.0 0.0 copy-start.2
  266.0 2.6 convert.1
  268.6 0.0 copy-done.3
  268.6 0.7 copy.40
  269.3 0.0 copy-done.2
  269.3 0.7 copy.41
Async XLA Ops:
  254.0 9.2 %copy-start.1 = (bf16[4,96,3072]{2,1,0:T(8,128)(2,1)S(1)}, bf16[4,96,3072]{2,1,0:T(8,128)(2,1)}, u32[]{:S(2)}) copy-start(bf16[4,96,3072]{2,1,0:T(8,128)(2,1)} %get-tuple-element.69) | copy-start | bytes 7077892
  263.2 2.8 %copy-start = (bf16[2,768,768]{2,1,0:T(8,128)(2,1)S(1)}, bf16[2,768,768]{2,1,0:T(8,128)(2,1)}, u32[]{:S(2)}) copy-start(bf16[2,768,768]{2,1,0:T(8,128)(2,1)} %get-tuple-element.71) | copy-start | bytes 7077892
  266.0 2.6 copy-start.3
  266.0 3.3 %copy-start.2 = (bf16[200,768]{1,0:T(8,128)(2,1)S(1)}, bf16[200,768]{1,0:T(8,128)(2,1)}, u32[]{:S(2)}) copy-start(bf16[200,768]{1,0:T(8,128)(2,1)} %get-tuple-element.65) | copy-start | bytes 921604
where the time goes:
time: 270 us
  Pallas kernels  251 us (93%)
  local copies, waits for them, and re-layouts  9.85 us (4%)
  other arithmetic  8.97 us (3%)
    pallas_call x1, Pallas kernels, back(): pl.pallas_call(functools.partial(back_kernel, planes, HEADS, own, groups,...  94.6 us
    pallas_call x1, Pallas kernels, experts_of_the_plane(): pl.pallas_call(functools.partial(expert_kernel, planes, own, rows, real),...  84.5 us
    pallas_call x1, Pallas kernels, front(): pl.pallas_call(functools.partial(front_kernel, planes, HEADS, real), out_...  71.4 us
    unnamed x14, local copies, waits for them, and re-layouts  5.6 us

commit v1 on v0

--- a/solution.py
+++ b/solution.py
@@ -1061,12 +1061,11 @@
             g_c(z + h, 0).start()
 
     line([1])
-    lined = [ref[...].astype(f32) for ref in vector_refs] + [outer_bias_ref[...].astype(f32)]
+    lined = [ref[...].astype(f32) for ref in (*vector_refs, outer_bias_ref, router_part_ref)]
     lined = jnp.concatenate(lined, axis=0)
     lined = jnp.concatenate([lined, jnp.zeros((128 - lined.shape[0], depth), f32)], axis=0)
     lined = jnp.concatenate([lined, jnp.zeros((128, 128 - depth), f32)], axis=1)
-    routed = jnp.concatenate([router_part_ref[...].astype(f32), jnp.zeros((depth, 128 - experts), f32)], axis=1)
-    small = jnp.transpose(lined)[:depth] + pltpu.roll(routed, 5 + experts, 1)
+    small = jnp.transpose(lined)[:depth]
     small_all[here_rows, :] = small.astype(bf16)
     line([0])
     w_proj_all[here_rows, :] = proj_part_ref[...]
@@ -1082,12 +1081,11 @@
     keep = jnp.sum(jnp.where(keep, keys, 0.0), axis=1, keepdims=True)
     keep_ref[...] = keep
     ids = ids_ref[...]
-    number = lax.broadcasted_iota(jnp.int32, (real, 128), 1)
-    select = ((number == ids[:, 0:1]) | (number == ids[:, 1:2])).astype(f32)
-    select = jnp.concatenate([select, jnp.zeros((rows - real, 128), f32)], axis=0)
-    select_ref[...] = select.astype(bf16)
-    chosen = jnp.transpose(jnp.concatenate([select, jnp.zeros((256 - rows, 128), f32)], axis=0))[:8]
-    chosen = jnp.concatenate([chosen, jnp.zeros((8, width - 256), f32)], axis=1)
+    number = lax.broadcasted_iota(jnp.int32, (8, real), 0)
+    chosen = ((number == ids[0:1]) | (number == ids[1:2])).astype(f32)
+    chosen = jnp.concatenate([chosen, jnp.zeros((8, width - real), f32)], axis=1)
+    select = jnp.concatenate([chosen[:, :256], jnp.zeros((120, 256), f32)], axis=0)
+    select_ref[...] = jnp.transpose(select)[:rows].astype(bf16)
     if rows - real > 8:
         chosen = jnp.concatenate([chosen, jnp.zeros((rows - real - 8, width), f32)], axis=0)
     grad_out = cotangent_ref[...].astype(f32) * keep[:real]
@@ -1726,7 +1724,9 @@
                 1 + group, :, part * group_width : (part + 1) * group_width
             ]
     arrived(small_at)
-    small_out[...] = final_small[...].astype(f32)
+    small_out[...] = jnp.transpose(
+        jnp.concatenate([final_small[...].astype(f32), jnp.zeros((128 - depth, 128), f32)], axis=0)
+    )
     outer_own.wait()
     outer_c().wait_recv()
     bias_theirs = bias_out.at[1 - c]
@@ -1806,7 +1806,7 @@
             shape((real, width), bf16),
             shape((depth, 3 * width), bf16),
             shape((depth, width), bf16),
-            shape((depth, 128), f32),
+            shape((128, 128), f32),
             shape((2 * own, depth, 2 * planes * lanes), bf16),
             shape((2, tall, width), bf16),
             shape((2, *bias_grad.shape), f32),
@@ -1852,6 +1852,75 @@
     )(*args)
 
 
+def finish_kernel(
+    depth,
+    experts,
+    qkv_ref,
+    proj_ref,
+    rows_ref,
+    inner_ref,
+    outer_ref,
+    mixed_ref,
+    token_grad_ref,
+    qkv_out,
+    proj_out,
+    inner_out,
+    outer_out,
+    mixed_out,
+    token_grad_out,
+    router_out,
+    outer_bias_out,
+    *vector_outs,
+):
+    f32 = jnp.float32
+
+    @pl.when(pl.program_id(0) == 0)
+    def _():
+        for i, out in enumerate(vector_outs):
+            out[...] = rows_ref[i : i + 1, :depth]
+        outer_bias_out[...] = rows_ref[8 : 8 + experts, :depth]
+        router_out[...] = rows_ref[16 : 16 + experts, :depth]
+        qkv_out[...] = qkv_ref[...].astype(f32)
+        proj_out[...] = proj_ref[...].astype(f32)
+        mixed_out[...] = mixed_ref[...]
+        token_grad_out[...] = token_grad_ref[...]
+
+    inner_out[...] = inner_ref[...].astype(f32)
+    outer_out[...] = outer_ref[...].astype(f32)
+
+
+def finish(qkv, proj, vectors, inner, outer, mixed, token_grad):
+    f32 = jnp.float32
+    experts, depth, _ = inner.shape
+    shape = jax.ShapeDtypeStruct
+
+    def whole(array):
+        return pl.BlockSpec(array.shape, lambda i, rank=len(array.shape): (0,) * rank)
+
+    def one(array):
+        return pl.BlockSpec((1, *array.shape[1:]), lambda i: (i, 0, 0))
+
+    outs = [
+        shape(qkv.shape, f32),
+        shape(proj.shape, f32),
+        shape(inner.shape, f32),
+        shape(outer.shape, f32),
+        shape(mixed.shape, mixed.dtype),
+        shape(token_grad.shape, token_grad.dtype),
+        shape((experts, depth), f32),
+        shape((experts, depth), f32),
+    ] + [shape((1, depth), f32)] * 5
+    return pl.pallas_call(
+        functools.partial(finish_kernel, depth, experts),
+        out_shape=outs,
+        grid=(experts,),
+        in_specs=[whole(qkv), whole(proj), whole(vectors), one(inner), one(outer), whole(mixed), whole(token_grad)],
+        out_specs=[whole(outs[0]), whole(outs[1]), one(outs[2]), one(outs[3])] + [whole(out) for out in outs[4:]],
+        compiler_params=pltpu.CompilerParams(vmem_limit_bytes=62 * 2**20),
+        name="results_in_float32",
+    )(qkv, proj, vectors, inner, outer, mixed, token_grad)
+
+
 def norm_parts(values):
     center = values - jnp.mean(values, axis=-1, keepdims=True)
     rstd = lax.rsqrt(jnp.mean(center * center, axis=-1, keepdims=True) + epsilon)
@@ -1898,10 +1967,10 @@
         padded,
         tokens[0],
         key_mask,
-        expert_ids[0],
+        expert_ids[0].T,
         cotangent[0],
         vectors,
-        w_router,
+        w_router.T,
         b_out,
         w_qkv,
         w_proj,
@@ -1936,21 +2005,25 @@
         bias_grad,
         router_grad,
     )
+    outer_grad = outer_grad.reshape(experts, slice_width, width)
+    finished = finish(qkv_grad, proj_grad, vector_grads, inner_grad, outer_grad, mixed, token_grad)
+    qkv_grad, proj_grad, inner_grad, outer_grad, mixed, token_grad, router_grad, outer_bias_grad = finished[:8]
+    vector_grads = [row.reshape(depth) for row in finished[8:]]
     return (
         mixed[None],
         token_grad[None],
-        vector_grads[:, 0],
-        vector_grads[:, 1],
-        qkv_grad.astype(f32),
-        proj_grad.astype(f32),
-        vector_grads[:, 2],
-        vector_grads[:, 3],
-        vector_grads[:, 4],
-        vector_grads[:, 16 : 16 + experts],
-        inner_grad.astype(f32),
+        vector_grads[0],
+        vector_grads[1],
+        qkv_grad,
+        proj_grad,
+        vector_grads[2],
+        vector_grads[3],
+        vector_grads[4],
+        router_grad.T,
+        inner_grad,
         bias_grad[:, 0].reshape(experts, slice_width),
-        outer_grad.reshape(experts, slice_width, width).astype(f32),
-        vector_grads[:, 8 : 8 + experts].T,
+        outer_grad,
+        outer_bias_grad,
     )
 
 

time: 270 us -> 261 us (0.967)
  other arithmetic: 8.97 us -> 0 us
  local copies, waits for them, and re-layouts: 9.85 us -> 1.44 us
  Pallas kernels: 251 us -> 258 us
    convert_element_type x4 -> x0, other arithmetic: 8.97 us -> none  [the longest x1 2.76 us: move_tokens_plan(): inner_grad.astype(f32)]
    pallas_call x0 -> x1, Pallas kernels: none -> 7.47 us  [finish(): pl.pallas_call(functools.partial(finish_kernel, depth, experts), out_shap...]
    unnamed x14 -> x0, local copies, waits for them, and re-layouts: 5.6 us -> none
where the time goes in v1:
time: 261 us; the launch traced here: 260 us
  Pallas kernels  258 us (99%)
    pallas_call x1, Pallas kernels, back(): pl.pallas_call(functools.partial(back_kernel, planes, HEADS, own, groups,...  94.6 us
    pallas_call x1, Pallas kernels, experts_of_the_plane(): pl.pallas_call(functools.partial(expert_kernel, planes, own, rows, real),...  84.5 us
    pallas_call x1, Pallas kernels, front(): pl.pallas_call(functools.partial(front_kernel, planes, HEADS, real), out_...  71.4 us
    pallas_call x1, Pallas kernels, finish(): pl.pallas_call(functools.partial(finish_kernel, depth, experts), out_shap...  7.47 us

profile of v1, /device:TPU:0, one launch (start us, length us, event | category | flops | bytes accessed | tf_op | source)
XLA Modules:
  0.0 260.3 jit_solution(5765723300216225357)
XLA Ops:
  0.7 71.4 %dense_weights_and_attention.1 = (bf16[768,128]{1,0:T(8,128)(2,1)}, bf16[768,2304]{1,0:T(8,128)(2,1)}, bf16[768,768]{1,0:T(8,128)(2,1)}, bf16[768,768]{1,0:T(8,1...) custom-call(bf16[200,768]{1,0:T(8,128)(2,1)} %bitcast.21, ...), custom_call_target="tpu_custom_call" | custom-call | flops 4294967296 | bytes 41943040 | tf_op jit(solution)/shard_map/dense_weights_and_attention/pallas_call | solution.py:1221
  72.1 84.5 %experts_of_the_plane.1 = (bf16[4,832,768]{2,1,0:T(8,128)(2,1)}, f32[208,768]{1,0:T(8,128)}, bf16[768,768]{1,0:T(8,128)(2,1)}, bf16[768,768]{1,0:T(8,128)(2,1)}, f32[8,768]{1,0:T(8,128)}, /*index=5*/f32[768,128]{1,0:T(8,128)}) custom-call(bf16[208,768]{1,0:T(8,128)(2,1)} %get-tuple-element.56.normed_ref.refs_1_, ...), custom_call_target="tpu_custom_call" | custom-call | flops 23555211264 | bytes 41943040 | tf_op jit(solution)/shard_map/experts_of_the_plane/pallas_call | solution.py:757
  156.6 94.6 %attention_backward_and_sums.1 = (bf16[200,768]{1,0:T(8,128)(2,1)}, bf16[200,768]{1,0:T(8,128)(2,1)}, bf16[96,2304]{1,0:T(8,128)(2,1)}, bf16[96,768]{1,0:T(8,128...) custom-call(f32[208,768]{1,0:T(8,128)} %get-tuple-element.60.refs_0_, ...), custom_call_target="tpu_custom_call" | custom-call | flops 8589934592 | bytes 41943040 | tf_op jit(solution)/shard_map/attention_backward_and_sums/pallas_call | solution.py:1802
  251.3 0.8 slice_reduce_fusion
  252.1 0.6 reshape_squeeze.3
  252.7 7.5 %results_in_float32.1 = (f32[96,2304]{1,0:T(8,128)}, f32[96,768]{1,0:T(8,128)}, f32[4,96,3072]{2,1,0:T(8,128)}, f32[4,384,768]{2,1,0:T(8,128)}, bf16[200,768]{1,...) custom-call(bf16[96,2304]{1,0:T(8,128)(2,1)} %get-tuple-element.77.q, ...), custom_call_target="tpu_custom_call" | custom-call | tf_op jit(solution)/shard_map/results_in_float32/pallas_call | solution.py:1913

commit v2 on v1

--- a/solution.py
+++ b/solution.py
@@ -416,6 +416,7 @@
     router_grad_ref,
     grads_ref,
     mix_ref,
+    mix_from_core,
     outer_ref,
     inner_t_ref,
     outer_t_ref,
@@ -434,6 +435,8 @@
     outer_sem,
     grads_sem,
     mix_sem,
+    mix_c_send,
+    mix_c_recv,
     z_send,
     z_recv,
     x_send,
@@ -524,12 +527,31 @@
     def grads_load(level):
         return pltpu.make_async_copy(grads_all_ref.at[level], grads_ref.at[level], grads_sem.at[level])
 
+    def mix_c(level, r):
+        return remote(
+            slot(mix_ref, level, 2 * r + 1),
+            slot(mix_from_core, level, r),
+            mix_c_send.at[level, r],
+            mix_c_recv.at[level, r],
+            place.other_core(),
+        )
+
     def mix_store(level, r):
-        here = pl.ds(pl.multiple_of(2 * r * rows, 16), 2 * rows)
-        return pltpu.make_async_copy(mix_ref.at[level, here], mix_out_ref.at[level, here], mix_sem.at[level, r])
+        return pltpu.make_async_copy(
+            slot(mix_ref, level, 2 * r), slot(mix_out_ref, level, r), mix_sem.at[level, r]
+        )
+
+    def mix_sum(level):
+        for r in range(2):
+            mix_c(level, r).wait_recv()
+            here = slice(2 * r * rows, (2 * r + 1) * rows)
+            total = mix_ref[level, here, :].astype(f32)
+            total = total + mix_from_core[level, r * rows : (r + 1) * rows, :].astype(f32)
+            mix_ref[level, here, :] = total.astype(bf16)
+            mix_store(level, r).start()
 
     for i in range(planes):
-        grads_load(nearest(place, i)).start()
+        grads_load(nearest(place, (i + 1) % planes)).start()
     loads = [
         pltpu.make_async_copy(
             outer_all_ref.at[c * own + i], outer_ref.at[pl.ds(i * lanes, lanes)], outer_sem.at[i]
@@ -646,73 +668,64 @@
         router_grad_ref[...] += lax.dot_general(tokens[level], logit_grad[...], TN, preferred_element_type=f32)
 
     def order(i):
-        return nearest(place, jnp.where(i == 0, 0, jnp.where(i == planes - 1, 1, i + 1)))
+        return nearest(place, jnp.where(i == 0, 1, jnp.where(i == planes - 1, 0, planes - i)))
 
     def step(i, carry):
         level, before = order(i), order(i - 1)
 
         def half(s, carry):
-            r = jnp.where(i == 0, s, 1 - s)
+            r = jnp.where(i < planes - 2, s, 1 - s)
 
             @pl.when((i == 0) & (s == 0))
             def _():
-                grads_load(z).wait()
-                c_copy(z, 0).wait_recv()
-
-            @pl.when((i == 0) & (s == 1))
+                hop(1)
+
+            if planes > 2:
+                @pl.when((i == 0) & (s == 1))
+                def _():
+                    hop(2)
+
+            @pl.when((i == 1) & (s == 0))
             def _():
-                hop(1)
-
-            @pl.when((i == 0) == (s == 1))
+                for h in range(3, planes):
+                    hop(h)
+
+            @pl.when((i > 0) & (s == 1))
+            def _():
+                level_sum(before)
+                sum_z_copy(before, z).start()
+
+            @pl.when(s == 0)
+            def _():
+                grads_load(level).wait()
+
+            @pl.when(r == 0)
+            def _():
+                c_copy(level, 0).wait_recv()
+
+            @pl.when(r == 1)
             def _():
                 x_copy(level).wait_recv()
                 c_copy(level, 1).start()
                 c_copy(level, 1).wait_recv()
 
-            @pl.when((i > 0) & (s == 0))
-            def _():
-                grads_load(level).wait()
-
-            @pl.when((i > 0) & (s == 1))
-            def _():
-                @pl.when(i + 2 < planes)
-                def _():
-                    hop(i + 2)
-
-                level_sum(before)
-
-                @pl.when(before != z)
-                def _():
-                    sum_z_copy(before, z).start()
-
-                across_sum(level)
-                c_copy(level, 0).wait_recv()
-
             tiles(level, r)
             sum_c_copy(level, r).start()
-            mix_store(level, r).start()
+            mix_c(level, r).start()
+
+            @pl.when(r == 1)
+            def _():
+                across_sum(level)
+
             return carry
 
         lax.fori_loop(0, 2, half, 0)
-
-        @pl.when((i == 0) & (i + 2 < planes))
-        def _():
-            hop(2)
-
-        @pl.when(i == planes - 1)
-        def _():
-            level_sum(level)
-            sum_z_copy(level, z).start()
-
         weight_grads(level)
-
-        @pl.when(i == 0)
-        def _():
-            across_sum(z)
-
+        mix_sum(level)
         return carry
 
     lax.fori_loop(0, planes, step, 0)
+    level_sum(z)
     inner_grad_ref[...] = inner_acc[...].astype(bf16)
     outer_grad_ref[...] = outer_acc[...].astype(bf16)
     total = part[z, 0:rows, :].astype(f32)
@@ -724,6 +737,8 @@
     for level in range(planes):
         mix_store(level, 0).wait()
         mix_store(level, 1).wait()
+        mix_c(level, 0).wait_send()
+        mix_c(level, 1).wait_send()
         x_copy(level).wait_send()
         c_copy(level, 0).wait_send()
         c_copy(level, 1).wait_send()
@@ -757,7 +772,7 @@
     return pl.pallas_call(
         functools.partial(expert_kernel, planes, own, rows, real),
         out_shape=[
-            shape((planes, chunk, width), bf16),
+            shape((planes, 2 * rows, width), bf16),
             shape((rows, width), f32),
             shape((width, units), bf16),
             shape((units, width), bf16),
@@ -769,6 +784,7 @@
         scratch_shapes=[
             pltpu.VMEM((planes, chunk, width), bf16),
             pltpu.VMEM((planes, chunk, width), bf16),
+            pltpu.VMEM((planes, 2 * rows, width), bf16),
             pltpu.VMEM((units, width), bf16),
             pltpu.VMEM((units, width), bf16),
             pltpu.VMEM((width, units), bf16),
@@ -786,6 +802,8 @@
             pltpu.VMEM((units, width), f32),
             dma((own,)),
             dma((planes,)),
+            dma((planes, 2)),
+            dma((planes, 2)),
             dma((planes, 2)),
         ]
         + [dma((2, planes))] * 2
@@ -1283,9 +1301,7 @@
         outer_sum,
         grad_attended,
         grad_qkv,
-        mix_x,
         mix_z,
-        mix_from_core,
         mix_from_x,
         mix_from_z,
         inner_from_y,
@@ -1306,12 +1322,10 @@
         from_y_small,
         final,
         final_small,
-    ) = refs[:27]
+    ) = refs[:25]
     (
         load_sem,
         outer_own_sem,
-        mix_c_send,
-        mix_c_recv,
         mix_x_send,
         mix_x_recv,
         mix_z_send,
@@ -1332,7 +1346,7 @@
         flow_z_recv,
         flow_y_sem,
         flow_end_sem,
-    ) = refs[27:]
+    ) = refs[25:]
     f32, bf16 = jnp.float32, jnp.bfloat16
     place = Place(planes)
     y, c, z, x = place.y, place.c, place.z, place.x
@@ -1422,41 +1436,26 @@
         flow_end(j).start()
 
     loads = [
-        pltpu.make_async_copy(mix_ref.at[:, pl.ds(2 * rows, rows)], mix_x, load_sem.at[0]),
-        pltpu.make_async_copy(mix_ref.at[:, pl.ds(0, rows)], mix_z, load_sem.at[1]),
-        pltpu.make_async_copy(w_qkv_all_ref, w_qkv_ref, load_sem.at[2]),
+        pltpu.make_async_copy(mix_ref.at[:, pl.ds(0, rows)], mix_z, load_sem.at[0]),
+        pltpu.make_async_copy(w_qkv_all_ref, w_qkv_ref, load_sem.at[1]),
     ]
 
-    def mix_c(r):
+    def mix_to_x(level):
         return remote(
-            mix_ref.at[:, pl.ds((2 * r + 1) * rows, rows)],
-            mix_from_core.at[:, pl.ds(r * rows, rows)],
-            mix_c_send.at[r],
-            mix_c_recv.at[r],
-            place.other_core(),
+            mix_ref.at[level, pl.ds(rows, rows)],
+            mix_from_x.at[level],
+            mix_x_send.at[level],
+            mix_x_recv.at[level],
+            place.other_x(),
         )
 
-    def mix_to_x(level):
-        return remote(mix_x.at[level], mix_from_x.at[level], mix_x_send.at[level], mix_x_recv.at[level], place.other_x())
+    def mix_start(k):
+        mix_to_x(lax.rem(z + k, planes)).start()
 
     def mix_to_z(level, source):
         return remote(
             mix_z.at[level], mix_from_z.at[source], mix_z_send.at[level], mix_z_recv.at[source], place.at(y, c, level, x)
         )
-
-    def mix_core_sum():
-        for load in loads[:2]:
-            load.wait()
-        mix_c(0).wait_recv()
-        mix_c(1).wait_recv()
-        for k in range(1, planes + 1):
-            level = lax.rem(z + k, planes)
-            total = mix_x[level].astype(f32) + mix_from_core[level, rows:, :].astype(f32)
-            mix_x[level] = total.astype(bf16)
-            mix_to_x(level).start()
-        for level in range(planes):
-            total = mix_z[level].astype(f32) + mix_from_core[level, :rows, :].astype(f32)
-            mix_z[level] = total.astype(bf16)
 
     def mix_x_sum(k):
         level = lax.rem(z + k, planes)
@@ -1546,8 +1545,7 @@
     greet(partners)
     inner_y().start()
     bias_y().start()
-    mix_c(1).start()
-    mix_c(0).start()
+    mix_start(1)
     for load in loads:
         load.start()
 
@@ -1583,7 +1581,7 @@
     grad_middle = grad_out.astype(f32) + norm_back(grad_normed_mid, normal_mid, rstd_mid, gain_second)
     grad_proj = grad_middle.astype(bf16)
     proj_bias_grad = jnp.sum(grad_proj.astype(f32), axis=0, keepdims=True)
-    mix_core_sum()
+    loads[0].wait()
 
     def hold(j, value):
         held[j] = value.astype(bf16).reshape(planes, 2, depth, width)
@@ -1641,6 +1639,7 @@
         )
 
     group_back(0)
+    mix_start(2)
     inner_y_sum()
     flow_core_sum(1)
     mix_x_sum(1)
@@ -1648,9 +1647,13 @@
         group_back(group)
         flow_core_sum(1 + group)
         if group == 1:
+            flow_x_sum(0)
             mix_x_sum(2)
-
-    loads[2].wait()
+    if groups == 1:
+        flow_x_sum(0)
+        mix_x_sum(2)
+
+    loads[1].wait()
     grad_normed_in = jnp.zeros((rows, width), f32)
     for group in range(groups):
         for part in range(3):
@@ -1682,17 +1685,25 @@
     held_small[...] = vector_grads.astype(bf16).reshape(planes, 2, depth, 128)
     flow_c(small_at).start()
     flow_core_sum(small_at)
+    inner_spread_done()
+    for group in range(groups - 1):
+        flow_x_sum(1 + group)
+    mix_start(3)
+    flow_x_sum(groups)
+    for k in range(4, planes + 1):
+        mix_start(k)
+    flow_x_sum(small_at)
+    outer_y_sum()
     for k in range(3, planes):
         mix_x_sum(k)
-    inner_spread_done()
-    flow_x_sum(0)
-    flow_x_sum(1)
+    flow_z_sum(0)
+    flow_y_sum(0)
+    for group in range(groups):
+        flow_z_sum(1 + group)
+    flow_z_sum(small_at)
+    inner_back().wait_recv()
+    inner_core(their_expert, 1).start()
     mix_x_sum(planes)
-    outer_y_sum()
-    for group in range(1, groups):
-        flow_x_sum(1 + group)
-    flow_z_sum(0)
-    flow_x_sum(small_at)
     mixture = mix_z[z].astype(f32) + dot(gates.astype(bf16), jnp.transpose(outer_bias.astype(f32)).astype(bf16))
     for k in range(1, planes):
         source = lax.rem(z + k, planes)
@@ -1700,12 +1711,6 @@
         mixture = mixture + mix_from_z[source].astype(f32)
     mixed = (keep_ref[...] * (middle_ref[...] + mixture)).astype(bf16)
     mixed_ref[...] = mixed[:real]
-    flow_y_sum(0)
-    for group in range(groups):
-        flow_z_sum(1 + group)
-    flow_z_sum(small_at)
-    inner_back().wait_recv()
-    inner_core(their_expert, 1).start()
     for group in range(groups):
         flow_y_sum(1 + group)
     flow_y_sum(small_at)
@@ -1734,8 +1739,6 @@
     for at, expert in enumerate(((1 - c) * 2 + y, (1 - c) * 2 + 1 - y)):
         inner_core(expert, at).wait_recv()
 
-    mix_c(0).wait_send()
-    mix_c(1).wait_send()
     inner_y().wait_send()
     inner_back().wait_send()
     inner_core(my_expert, 0).wait_send()
@@ -1820,8 +1823,6 @@
             pltpu.VMEM((groups, rows, 3 * width // groups), bf16),
             pltpu.VMEM((planes, rows, width), bf16),
             pltpu.VMEM((planes, rows, width), bf16),
-            pltpu.VMEM((planes, 2 * rows, width), bf16),
-            pltpu.VMEM((planes, rows, width), bf16),
             pltpu.VMEM((planes, rows, width), bf16),
             pltpu.VMEM((width, lanes), bf16),
             pltpu.VMEM((width, lanes), bf16),
@@ -1835,8 +1836,7 @@
         + both(half)
         + both(half)
         + both(depth)
-        + [dma((3,)), dma]
-        + [dma((2,))] * 2
+        + [dma((2,)), dma]
         + [dma((planes,))] * 4
         + [dma((2,))]
         + [dma((planes, 2))] * 2
@@ -2035,7 +2035,7 @@
         experts, _, hidden = w_in.shape
         lanes = hidden // n_fsdp
         whole_tiles = lanes % 128 == 0 and tokens.shape[2] % 256 == 0 and w_in.shape[1] % 32 == 0 and 2 * lanes <= tokens.shape[2]
-        if n_seq == 4 and experts == n_seq and tokens.shape[0] == 1 and whole_tiles:
+        if n_seq == 4 and experts == n_seq and n_fsdp >= 6 and n_fsdp % 2 == 0 and tokens.shape[0] == 1 and whole_tiles:
             return move_tokens_plan(*args)
         return gather_weights_plan(*args)
 

time: 261 us -> 258 us (0.989); the launches traced: 260 us -> 253 us
  Pallas kernels: 258 us -> 251 us
    pallas_call x1, Pallas kernels: 84.5 us -> 80.9 us  [experts_of_the_plane(): pl.pallas_call(functools.partial(expert_kernel, planes, own, rows, real),...]
    pallas_call x1, Pallas kernels: 94.6 us -> 91.2 us  [back(): pl.pallas_call(functools.partial(back_kernel, planes, HEADS, own, groups,...]
where the time goes in v2:
time: 258 us; the launch traced here: 253 us
  Pallas kernels  251 us (97%)
    pallas_call x1, Pallas kernels, back(): pl.pallas_call(functools.partial(back_kernel, planes, HEADS, own, groups,...  91.2 us
    pallas_call x1, Pallas kernels, experts_of_the_plane(): pl.pallas_call(functools.partial(expert_kernel, planes, own, rows, real),...  80.9 us
    pallas_call x1, Pallas kernels, front(): pl.pallas_call(functools.partial(front_kernel, planes, HEADS, real), out_...  71.4 us
    pallas_call x1, Pallas kernels, finish(): pl.pallas_call(functools.partial(finish_kernel, depth, experts), out_shap...  7.47 us

profile of v2, /device:TPU:0, one launch (start us, length us, event | category | flops | bytes accessed | tf_op | source)
XLA Modules:
  0.0 253.2 jit_solution(7524348610205996110)
XLA Ops:
  0.7 71.4 %dense_weights_and_attention.1 = (bf16[768,128]{1,0:T(8,128)(2,1)}, bf16[768,2304]{1,0:T(8,128)(2,1)}, bf16[768,768]{1,0:T(8,128)(2,1)}, bf16[768,768]{1,0:T(8,1...) custom-call(bf16[200,768]{1,0:T(8,128)(2,1)} %bitcast.21, ...), custom_call_target="tpu_custom_call" | custom-call | flops 4294967296 | bytes 41943040 | tf_op jit(solution)/shard_map/dense_weights_and_attention/pallas_call | solution.py:1239
  72.0 80.9 %experts_of_the_plane.1 = (bf16[4,416,768]{2,1,0:T(8,128)(2,1)}, f32[208,768]{1,0:T(8,128)}, bf16[768,768]{1,0:T(8,128)(2,1)}, bf16[768,768]{1,0:T(8,128)(2,1)}, f32[8,768]{1,0:T(8,128)}, /*index=5*/f32[768,128]{1,0:T(8,128)}) custom-call(bf16[208,768]{1,0:T(8,128)(2,1)} %get-tuple-element.56.normed_ref.refs_1_, ...), custom_call_target="tpu_custom_call" | custom-call | flops 23555211264 | bytes 41943040 | tf_op jit(solution)/shard_map/experts_of_the_plane/pallas_call | solution.py:772
  152.9 91.2 %attention_backward_and_sums.1 = (bf16[200,768]{1,0:T(8,128)(2,1)}, bf16[200,768]{1,0:T(8,128)(2,1)}, bf16[96,2304]{1,0:T(8,128)(2,1)}, bf16[96,768]{1,0:T(8,128...) custom-call(f32[208,768]{1,0:T(8,128)} %get-tuple-element.60.refs_0_, ...), custom_call_target="tpu_custom_call" | custom-call | flops 8589934592 | bytes 41943040 | tf_op jit(solution)/shard_map/attention_backward_and_sums/pallas_call | solution.py:1805
  244.2 0.8 slice_reduce_fusion
  245.0 0.6 reshape_squeeze.3
  245.6 7.5 %results_in_float32.1 = (f32[96,2304]{1,0:T(8,128)}, f32[96,768]{1,0:T(8,128)}, f32[4,96,3072]{2,1,0:T(8,128)}, f32[4,384,768]{2,1,0:T(8,128)}, bf16[200,768]{1,...) custom-call(bf16[96,2304]{1,0:T(8,128)(2,1)} %get-tuple-element.77.q, ...), custom_call_target="tpu_custom_call" | custom-call | tf_op jit(solution)/shard_map/results_in_float32/pallas_call | solution.py:1913

commit v3 on v2

--- a/solution.py
+++ b/solution.py
@@ -1862,6 +1862,7 @@
     outer_ref,
     mixed_ref,
     token_grad_ref,
+    bias_ref,
     qkv_out,
     proj_out,
     inner_out,
@@ -1870,6 +1871,7 @@
     token_grad_out,
     router_out,
     outer_bias_out,
+    bias_out,
     *vector_outs,
 ):
     f32 = jnp.float32
@@ -1882,6 +1884,10 @@
         router_out[...] = rows_ref[16 : 16 + experts, :depth]
         qkv_out[...] = qkv_ref[...].astype(f32)
         proj_out[...] = proj_ref[...].astype(f32)
+        lanes = bias_out.shape[1]
+        for e in range(experts):
+            at = e % (experts // 2) * lanes
+            bias_out[e : e + 1, :] = bias_ref[e // (experts // 2), 0:1, at : at + lanes]
         mixed_out[...] = mixed_ref[...]
         token_grad_out[...] = token_grad_ref[...]
 
@@ -1889,7 +1895,7 @@
     outer_out[...] = outer_ref[...].astype(f32)
 
 
-def finish(qkv, proj, vectors, inner, outer, mixed, token_grad):
+def finish(qkv, proj, vectors, inner, outer, mixed, token_grad, bias):
     f32 = jnp.float32
     experts, depth, _ = inner.shape
     shape = jax.ShapeDtypeStruct
@@ -1909,16 +1915,18 @@
         shape(token_grad.shape, token_grad.dtype),
         shape((experts, depth), f32),
         shape((experts, depth), f32),
+        shape((experts, outer.shape[1]), f32),
     ] + [shape((1, depth), f32)] * 5
     return pl.pallas_call(
         functools.partial(finish_kernel, depth, experts),
         out_shape=outs,
         grid=(experts,),
-        in_specs=[whole(qkv), whole(proj), whole(vectors), one(inner), one(outer), whole(mixed), whole(token_grad)],
+        in_specs=[whole(qkv), whole(proj), whole(vectors), one(inner), one(outer)]
+        + [whole(mixed), whole(token_grad), whole(bias)],
         out_specs=[whole(outs[0]), whole(outs[1]), one(outs[2]), one(outs[3])] + [whole(out) for out in outs[4:]],
         compiler_params=pltpu.CompilerParams(vmem_limit_bytes=62 * 2**20),
         name="results_in_float32",
-    )(qkv, proj, vectors, inner, outer, mixed, token_grad)
+    )(qkv, proj, vectors, inner, outer, mixed, token_grad, bias)
 
 
 def norm_parts(values):
@@ -2006,9 +2014,12 @@
         router_grad,
     )
     outer_grad = outer_grad.reshape(experts, slice_width, width)
-    finished = finish(qkv_grad, proj_grad, vector_grads, inner_grad, outer_grad, mixed, token_grad)
+    finished = finish(
+        qkv_grad, proj_grad, vector_grads, inner_grad, outer_grad, mixed, token_grad, bias_grad
+    )
     qkv_grad, proj_grad, inner_grad, outer_grad, mixed, token_grad, router_grad, outer_bias_grad = finished[:8]
-    vector_grads = [row.reshape(depth) for row in finished[8:]]
+    bias_grad = finished[8]
+    vector_grads = [row.reshape(depth) for row in finished[9:]]
     return (
         mixed[None],
         token_grad[None],
@@ -2021,7 +2032,7 @@
         vector_grads[4],
         router_grad.T,
         inner_grad,
-        bias_grad[:, 0].reshape(experts, slice_width),
+        bias_grad,
         outer_grad,
         outer_bias_grad,
     )

time: 258 us -> 257 us (level)
  no operation moved by 1% of the time
where the time goes in v3:
time: 257 us; the launch traced here: 252 us
  Pallas kernels  251 us (98%)
    pallas_call x1, Pallas kernels, back(): pl.pallas_call(functools.partial(back_kernel, planes, HEADS, own, groups,...  91.2 us
    pallas_call x1, Pallas kernels, experts_of_the_plane(): pl.pallas_call(functools.partial(expert_kernel, planes, own, rows, real),...  80.9 us
    pallas_call x1, Pallas kernels, front(): pl.pallas_call(functools.partial(front_kernel, planes, HEADS, real), out_...  71.4 us
    pallas_call x1, Pallas kernels, finish(): pl.pallas_call(functools.partial(finish_kernel, depth, experts), out_shap...  7.52 us

profile of v3, /device:TPU:0, one launch (start us, length us, event | category | flops | bytes accessed | tf_op | source)
XLA Modules:
  0.0 251.9 jit_solution(13204110748195645311)
XLA Ops:
  0.7 71.4 %dense_weights_and_attention.1 = (bf16[768,128]{1,0:T(8,128)(2,1)}, bf16[768,2304]{1,0:T(8,128)(2,1)}, bf16[768,768]{1,0:T(8,128)(2,1)}, bf16[768,768]{1,0:T(8,1...) custom-call(bf16[200,768]{1,0:T(8,128)(2,1)} %bitcast.21, ...), custom_call_target="tpu_custom_call" | custom-call | flops 4294967296 | bytes 41943040 | tf_op jit(solution)/shard_map/dense_weights_and_attention/pallas_call | solution.py:1239
  72.1 80.9 %experts_of_the_plane.1 = (bf16[4,416,768]{2,1,0:T(8,128)(2,1)}, f32[208,768]{1,0:T(8,128)}, bf16[768,768]{1,0:T(8,128)(2,1)}, bf16[768,768]{1,0:T(8,128)(2,1)}, f32[8,768]{1,0:T(8,128)}, /*index=5*/f32[768,128]{1,0:T(8,128)}) custom-call(bf16[208,768]{1,0:T(8,128)(2,1)} %get-tuple-element.57.normed_ref.refs_1_, ...), custom_call_target="tpu_custom_call" | custom-call | flops 23555211264 | bytes 41943040 | tf_op jit(solution)/shard_map/experts_of_the_plane/pallas_call | solution.py:772
  153.0 91.2 %attention_backward_and_sums.1 = (bf16[200,768]{1,0:T(8,128)(2,1)}, bf16[200,768]{1,0:T(8,128)(2,1)}, bf16[96,2304]{1,0:T(8,128)(2,1)}, bf16[96,768]{1,0:T(8,128...) custom-call(f32[208,768]{1,0:T(8,128)} %get-tuple-element.61.refs_0_, ...), custom_call_target="tpu_custom_call" | custom-call | flops 8589934592 | bytes 41943040 | tf_op jit(solution)/shard_map/attention_backward_and_sums/pallas_call | solution.py:1805
  244.2 7.5 %results_in_float32.1 = (f32[96,2304]{1,0:T(8,128)}, f32[96,768]{1,0:T(8,128)}, f32[4,96,3072]{2,1,0:T(8,128)}, f32[4,384,768]{2,1,0:T(8,128)}, bf16[200,768]{1,...) custom-call(bf16[96,2304]{1,0:T(8,128)(2,1)} %get-tuple-element.78.q, ...), custom_call_target="tpu_custom_call" | custom-call | tf_op jit(solution)/shard_map/results_in_float32/pallas_call | solution.py:1920

commit v4 on v3

--- a/solution.py
+++ b/solution.py
@@ -1904,7 +1904,7 @@
         return pl.BlockSpec(array.shape, lambda i, rank=len(array.shape): (0,) * rank)
 
     def one(array):
-        return pl.BlockSpec((1, *array.shape[1:]), lambda i: (i, 0, 0))
+        return pl.BlockSpec((1, array.shape[1] // 2, array.shape[2]), lambda i: (i // 2, i % 2, 0))
 
     outs = [
         shape(qkv.shape, f32),
@@ -1920,7 +1920,7 @@
     return pl.pallas_call(
         functools.partial(finish_kernel, depth, experts),
         out_shape=outs,
-        grid=(experts,),
+        grid=(2 * experts,),
         in_specs=[whole(qkv), whole(proj), whole(vectors), one(inner), one(outer)]
         + [whole(mixed), whole(token_grad), whole(bias)],
         out_specs=[whole(outs[0]), whole(outs[1]), one(outs[2]), one(outs[3])] + [whole(out) for out in outs[4:]],

time: 257 us -> 258 us (level)
  no operation moved by 1% of the time
where the time goes in v4:
time: 258 us; the launch traced here: 253 us
  Pallas kernels  252 us (98%)
    pallas_call x1, Pallas kernels, back(): pl.pallas_call(functools.partial(back_kernel, planes, HEADS, own, groups,...  91.2 us
    pallas_call x1, Pallas kernels, experts_of_the_plane(): pl.pallas_call(functools.partial(expert_kernel, planes, own, rows, real),...  80.9 us
    pallas_call x1, Pallas kernels, front(): pl.pallas_call(functools.partial(front_kernel, planes, HEADS, real), out_...  71.4 us
    pallas_call x1, Pallas kernels, finish(): pl.pallas_call(functools.partial(finish_kernel, depth, experts), out_shap...  8.72 us

profile of v4, /device:TPU:0, one launch (start us, length us, event | category | flops | bytes accessed | tf_op | source)
XLA Modules:
  0.0 253.1 jit_solution(15304365983566296096)
XLA Ops:
  0.7 71.4 %dense_weights_and_attention.1 = (bf16[768,128]{1,0:T(8,128)(2,1)}, bf16[768,2304]{1,0:T(8,128)(2,1)}, bf16[768,768]{1,0:T(8,128)(2,1)}, bf16[768,768]{1,0:T(8,1...) custom-call(bf16[200,768]{1,0:T(8,128)(2,1)} %bitcast.21, ...), custom_call_target="tpu_custom_call" | custom-call | flops 4294967296 | bytes 41943040 | tf_op jit(solution)/shard_map/dense_weights_and_attention/pallas_call | solution.py:1239
  72.1 80.9 %experts_of_the_plane.1 = (bf16[4,416,768]{2,1,0:T(8,128)(2,1)}, f32[208,768]{1,0:T(8,128)}, bf16[768,768]{1,0:T(8,128)(2,1)}, bf16[768,768]{1,0:T(8,128)(2,1)}, f32[8,768]{1,0:T(8,128)}, /*index=5*/f32[768,128]{1,0:T(8,128)}) custom-call(bf16[208,768]{1,0:T(8,128)(2,1)} %get-tuple-element.57.normed_ref.refs_1_, ...), custom_call_target="tpu_custom_call" | custom-call | flops 23555211264 | bytes 41943040 | tf_op jit(solution)/shard_map/experts_of_the_plane/pallas_call | solution.py:772
  153.0 91.2 %attention_backward_and_sums.1 = (bf16[200,768]{1,0:T(8,128)(2,1)}, bf16[200,768]{1,0:T(8,128)(2,1)}, bf16[96,2304]{1,0:T(8,128)(2,1)}, bf16[96,768]{1,0:T(8,128...) custom-call(f32[208,768]{1,0:T(8,128)} %get-tuple-element.61.refs_0_, ...), custom_call_target="tpu_custom_call" | custom-call | flops 8589934592 | bytes 41943040 | tf_op jit(solution)/shard_map/attention_backward_and_sums/pallas_call | solution.py:1805
  244.2 8.7 %results_in_float32.1 = (f32[96,2304]{1,0:T(8,128)}, f32[96,768]{1,0:T(8,128)}, f32[4,96,3072]{2,1,0:T(8,128)}, f32[4,384,768]{2,1,0:T(8,128)}, bf16[200,768]{1,...) custom-call(bf16[96,2304]{1,0:T(8,128)(2,1)} %get-tuple-element.78.q, ...), custom_call_target="tpu_custom_call" | custom-call | tf_op jit(solution)/shard_map/results_in_float32/pallas_call | solution.py:1920
